TPU v7x, 256 devices: a whole 4x4x8 slice. The times are simulated.
256 devices in a mesh: depth: 8 (over z_lo, y), row: 8 (over z_hi, core), col: 4 (over x).
Axes of the slice: x: 4, y: 4, z: 8 (z_hi: 4, z_lo: 2; z = z_hi * 2 + z_lo), core: 2. Of those that a mesh axis runs over, the one named last changes fastest.
Arguments:
- tokens: bfloat16 [768, 6144], P(('depth', 'col'), 'row'), may hold values from -6 to 6
- cotangent: bfloat16 [768, 6144], P(('depth', 'col'), 'row'), may hold values from -6 to 6
- gate_weight: bfloat16 [6144, 24576], P('row', ('depth', 'col')), may hold values from -0.078125 to 0.078125
- up_weight: bfloat16 [6144, 24576], P('row', ('depth', 'col')), may hold values from -0.078125 to 0.078125
- down_weight: bfloat16 [24576, 6144], P(('depth', 'col'), 'row'), may hold values from -0.0390625 to 0.0390625
Outputs:
- output: bfloat16 [768, 6144], P(('depth', 'col'), 'row')
- grad_tokens: bfloat16 [768, 6144], P(('depth', 'col'), 'row')
- grad_gate: bfloat16 [6144, 24576], P('row', ('depth', 'col'))
- grad_up: bfloat16 [6144, 24576], P('row', ('depth', 'col'))
- grad_down: bfloat16 [24576, 6144], P(('depth', 'col'), 'row')
All inputs are finite; a program needn't handle non-finite values.
Results may differ from a plain program's by a relative error of at most 0.005.
Values may be sent and summed in bfloat16 or wider, within the bound.
A program may use at most 64 MiB of HBM per device.

v0:
```python
import jax
import jax.numpy as jnp
from jax import lax
from jax.sharding import PartitionSpec as P


def down_back(rows_in, down_weight):
    return jnp.einsum("td,fd->tf", rows_in, down_weight, preferred_element_type=jnp.float32)


def hidden_from(gate_value, up_value):
    sigmoid_gate = jax.nn.sigmoid(gate_value)
    activated = gate_value * sigmoid_gate
    return (activated * up_value).astype(jnp.bfloat16)


def gate_slopes(slope_value, gate_value, up_value):
    sigmoid_gate = jax.nn.sigmoid(gate_value)
    activated = gate_value * sigmoid_gate
    gate_slope = (
        slope_value * up_value * sigmoid_gate * (1.0 + gate_value * (1.0 - sigmoid_gate))
    ).astype(jnp.bfloat16)
    up_slope = (slope_value * activated).astype(jnp.bfloat16)
    return (gate_slope, up_slope)


def local(tokens, cotangent, gate_weight, up_weight, down_weight):
    shard_rows = lax.all_gather(tokens, ("depth", "col"), axis=0, tiled=True)
    gathered_tokens = shard_rows
    gate_part = jnp.dot(shard_rows, gate_weight, preferred_element_type=jnp.float32)
    up_part = jnp.dot(shard_rows, up_weight, preferred_element_type=jnp.float32)
    gate_value, up_value = lax.psum((gate_part, up_part), "row")
    hidden = hidden_from(gate_value, up_value)
    output = lax.psum_scatter(
        jnp.dot(hidden, down_weight, preferred_element_type=jnp.float32),
        ("depth", "col"),
        scatter_dimension=0,
        tiled=True,
    ).astype(jnp.bfloat16)
    shard_rows = lax.all_gather(cotangent, ("depth", "col"), axis=0, tiled=True)
    slope_part = down_back(shard_rows, down_weight)
    slope_value = lax.psum(slope_part, "row")
    gate_slope, up_slope = gate_slopes(slope_value, gate_value, up_value)
    first_part = jnp.einsum(
        "tf,df->td", gate_slope, gate_weight, preferred_element_type=jnp.float32
    )
    second_part = jnp.einsum("tf,df->td", up_slope, up_weight, preferred_element_type=jnp.float32)
    grad_tokens = lax.psum_scatter(
        first_part + second_part, ("depth", "col"), scatter_dimension=0, tiled=True
    ).astype(jnp.bfloat16)
    grad_scale = gathered_tokens.shape[0] ** (-0.5)
    grad_gate = (
        jnp.einsum("td,tf->df", gathered_tokens, gate_slope, preferred_element_type=jnp.float32)
        * grad_scale
    ).astype(jnp.bfloat16)
    grad_up = (
        jnp.einsum("td,tf->df", gathered_tokens, up_slope, preferred_element_type=jnp.float32)
        * grad_scale
    ).astype(jnp.bfloat16)
    grad_down = (
        jnp.einsum("tf,td->fd", hidden, shard_rows, preferred_element_type=jnp.float32) * grad_scale
    ).astype(jnp.bfloat16)
    return (output, grad_tokens, grad_gate, grad_up, grad_down)


def solution(mesh):
    placed = (
        P(("depth", "col"), "row"),
        P(("depth", "col"), "row"),
        P("row", ("depth", "col")),
        P("row", ("depth", "col")),
        P(("depth", "col"), "row"),
    )
    return jax.shard_map(
        local,
        mesh=mesh,
        in_specs=placed,
        out_specs=(
            P(("depth", "col"), "row"),
            P(("depth", "col"), "row"),
            P("row", ("depth", "col")),
            P("row", ("depth", "col")),
            P(("depth", "col"), "row"),
        ),
        check_vma=False,
    )
```

profile of v0, /device:TPU:32, one launch (start us, length us, event | category | flops | bytes accessed | tf_op | source)
XLA Modules:
  0.0 842.0 jit_solution(10564383168859920260)
XLA Ops:
  7.2 0.0 copy-start
  7.2 0.0 all-gather.3.cloned.1.call-start
  7.2 0.7 all-gather.3.cloned.1.call-update
  7.9 0.0 all-gather.5.cloned.1.call-start
  8.0 0.7 all-gather.5.cloned.1.call-update
  8.7 0.0 copy-start.5
  8.7 0.0 all-reduce.3.cloned.1.call-start
  8.7 157.3 %all-gather.3.cloned.1.call-done = bf16[768,768]{1,0:T(8,128)(2,1)} async-done(((bf16[24,768]{1,0:T(8,128)(2,1)}), bf16[768,768]{1,0:T(8,128)(2,1)}) %all-gather.3.cloned.1.call-update) | async-done | bytes 1179664 | tf_op jit(solution)/shard_map/all_gather | solution.py:28
  166.0 0.0 copy-start.6
  166.0 4.3 fusion.4
  170.3 0.0 copy-done.5
  170.3 0.0 copy-done.6
  170.3 2.5 fusion.3
  172.8 149.5 %all-gather.5.cloned.1.call-done = bf16[768,768]{1,0:T(8,128)(2,1)} async-done(((bf16[24,768]{1,0:T(8,128)(2,1)}), bf16[768,768]{1,0:T(8,128)(2,1)}) %all-gather.5.cloned.1.call-update) | async-done | bytes 1179664 | tf_op jit(solution)/shard_map/all_gather | solution.py:40
  322.3 0.0 copy-done
  322.3 3.9 fusion.6
  326.2 0.0 all-reduce.3.cloned.1.call-update
  326.2 0.0 reduce-scatter.3.cloned.1.call-start
  326.3 167.9 %all-reduce.3.cloned.1.call-done = (f32[768,768]{1,0:T(8,128)}, f32[768,768]{1,0:T(8,128)}, f32[768,768]{1,0:T(8,128)}) async-done(((f32[768,768]{1,0:T(8,128)}, f32[768,768]{1,0:T(8,128)}, f32[768,768]{1,0:T(8,128)}), (f32[768,768]{1,0:T(8,128)}, f32[768,768]{1,0:T(8,128)}, f32[768,768]{1,0:T(8,128)})) %all-reduce.3.cloned.1.call-update) | async-done | bytes 7077904 | tf_op jit(solution)/shard_map/psum | solution.py:32
  494.2 4.4 multiply_convert_fusion.3
  498.6 0.0 copy-start.2
  498.6 0.0 copy-start.4
  498.6 1.0 copy-done.2
  499.6 2.5 fusion.5
  502.1 0.0 reduce-scatter.3.cloned.1.call-update
  502.2 0.0 reduce-scatter.5.cloned.1.call-start
  502.2 0.0 copy-done.4
  502.2 0.0 copy-start.1
  502.2 2.5 fusion.7
  504.7 0.0 copy-done.1
  504.7 2.6 convolution_add_fusion
  507.3 0.0 reduce-scatter.5.cloned.1.call-update
  507.3 2.7 fusion.1
  510.1 1.5 copy.10
  511.5 2.4 fusion.2
  513.9 0.0 copy-start.3
  513.9 1.5 copy.11
  515.4 0.0 copy-done.3
  515.4 3.4 multiply_convert_fusion
  518.8 149.4 %reduce-scatter.3.cloned.1.call-done = f32[24,768]{1,0:T(8,128)} async-done(((f32[768,768]{1,0:T(8,128)}), f32[24,768]{1,0:T(8,128)}) %reduce-scatter.3.cloned.1.call-update) | async-done | bytes 73744 | tf_op jit(solution)/shard_map/reduce_scatter | solution.py:34
  668.2 1.5 convert_element_type.31
  669.8 164.2 %reduce-scatter.5.cloned.1.call-done = f32[24,768]{1,0:T(8,128)} async-done(((f32[768,768]{1,0:T(8,128)}), f32[24,768]{1,0:T(8,128)}) %reduce-scatter.5.cloned.1.call-update) | async-done | bytes 73744 | tf_op jit(solution)/shard_map/reduce_scatter | solution.py:48
  833.9 1.5 convert_element_type.34
Async XLA Ops:
  7.2 315.2 %copy-start = (bf16[768,768]{1,0:T(8,128)(2,1)S(1)}, bf16[768,768]{1,0:T(8,128)(2,1)}, u32[]{:S(2)}) copy-start(bf16[768,768]{1,0:T(8,128)(2,1)} %param.9) | copy-start | bytes 3538948
  7.2 158.8 %all-gather.3.cloned.1.call-start = ((), (), s32[]{:S(2)}) async-start(), calls=%async_computation.2 | async-start | bytes 1216512 | tf_op jit(solution)/shard_map/all_gather | solution.py:28
  7.9 314.4 %all-gather.5.cloned.1.call-start = ((), (), s32[]{:S(2)}) async-start(), calls=%async_computation.4 | async-start | bytes 1216512 | tf_op jit(solution)/shard_map/all_gather | solution.py:40
  8.7 161.6 %copy-start.5 = (bf16[768,768]{1,0:T(8,128)(2,1)S(1)}, bf16[768,768]{1,0:T(8,128)(2,1)}, u32[]{:S(2)}) copy-start(bf16[768,768]{1,0:T(8,128)(2,1)} %param.7) | copy-start | bytes 3538948
  8.7 485.5 %all-reduce.3.cloned.1.call-start = ((), (), s32[]{:S(2)}) async-start(), calls=%async_computation.6 | async-start | bytes 14155776 | tf_op jit(solution)/shard_map/psum | solution.py:32
  166.0 4.3 copy-start.6
  326.2 342.0 %reduce-scatter.3.cloned.1.call-start = ((), (), s32[]{:S(2)}) async-start(), calls=%async_computation.3 | async-start | bytes 2433024 | tf_op jit(solution)/shard_map/reduce_scatter | solution.py:34
  498.6 1.0 copy-start.2
  498.6 3.6 copy-start.4
  502.2 331.8 %reduce-scatter.5.cloned.1.call-start = ((), (), s32[]{:S(2)}) async-start(), calls=%async_computation.5 | async-start | bytes 2433024 | tf_op jit(solution)/shard_map/reduce_scatter | solution.py:48
  502.2 2.5 copy-start.1
  513.9 1.5 copy-start.3
Sparse Core Ops, SparseCore 0:
  9.8 156.1 all-gather.2
  167.8 154.4 all-gather.4
  326.3 167.8 all-reduce.2
  502.3 165.9 reduce-scatter.2
  670.6 163.2 reduce-scatter.4
where the time goes:
time: 843 us; the launch traced here: 842 us
  waiting for transfers between devices  790 us (94%)
  matrix products  26.8 us (3%)
  between operations  13.9 us (2%)
    psum x1, waiting for transfers between devices, local(): gate_value, up_value = lax.psum((gate_part, up_part), 'row')  168 us
    reduce_scatter x1, waiting for transfers between devices, local(): lax.psum_scatter(first_part + second_part, ('depth', 'col'), scatter_dime...  164 us
    all_gather x1, waiting for transfers between devices, local(): shard_rows = lax.all_gather(tokens, ('depth', 'col'), axis=0, tiled=True)  157 us
    all_gather x1, waiting for transfers between devices, local(): shard_rows = lax.all_gather(cotangent, ('depth', 'col'), axis=0, tiled=True)  150 us
    reduce_scatter x1, waiting for transfers between devices, local(): lax.psum_scatter(jnp.dot(hidden, down_weight, preferred_element_type=jnp....  149 us
  transfers between devices with their start and end apart: 5, of which 5 were waited for; matrix products, arithmetic and copies ran while one was open for 3% of the time, Pallas kernels for 0%

commit v1 on v0

v1 whole, which is shorter than its diff:
```python
import functools

import jax
import jax.numpy as jnp
from jax import lax
from jax.experimental import pallas as pl
from jax.experimental.pallas import tpu as pltpu
from jax.sharding import PartitionSpec as P

F32 = jnp.float32
BF16 = jnp.bfloat16
W = 768
HALF = W // 2
CHUNKS = 3
T = W // CHUNKS
PIECE = T // 4
ROWS = T // 16
LOCAL = 24

ZL, X1, C1, X2, C2, CORE, ZA, ZB, ZC, GN, GP, GF, GC, O1, G1, O2, G2, FIN = (
    0, 1, 4, 7, 10, 13, 16, 17, 18, 19, 20, 21, 22, 26, 29, 32, 35, 38)
COPIES = 39


def nt(a, b):
    return lax.dot_general(a, b, (((1,), (1,)), ((), ())), preferred_element_type=F32)


def nn(a, b):
    return jnp.dot(a, b, preferred_element_type=F32)


def tn(a, b):
    return lax.dot_general(a, b, (((0,), (0,)), ((), ())), preferred_element_type=F32)


def kernel(x_in, c_in, wg_hbm, wu_hbm, wd_hbm,
           out_ref, gt_ref, gg_hbm, gu_hbm, gd_hbm,
           wg, wu, wd, zsrc, zdst, xc, csnd, crcv, part, zsnd, zrcv, hid,
           pf, psnd, pown, p1rcv, sf, s1snd, s1own, p2rcv, fin, frcv, res,
           grads, ssem, rsem, lsem, gsem):
    depth, row, xx = lax.axis_index("depth"), lax.axis_index("row"), lax.axis_index("col")
    zl, y, zh, a = depth // 4, depth % 4, row // 2, row % 2
    nxt, prv, opp = (zh + 1 + 2 * a) % 4, (zh + 3 + 2 * a) % 4, (zh + 2) % 4

    def dev(zl_=zl, y_=y, zh_=zh, a_=a, x_=xx):
        return (zl_ * 4 + y_, zh_ * 2 + a_, x_)

    others = ([dev(zl_=1 - zl), dev(a_=1 - a), dev(zh_=nxt), dev(zh_=prv)]
              + [dev(x_=(xx + j) % 4) for j in (1, 2, 3)]
              + [dev(y_=(y + j) % 4) for j in (1, 2, 3)])
    mine = pl.ds(pl.multiple_of(a * HALF, 128), HALF)
    theirs = pl.ds(pl.multiple_of((1 - a) * HALF, 128), HALF)
    copies = {}

    def send(i, k, src, dst, to):
        copies[i, k] = pltpu.make_async_remote_copy(
            src_ref=src, dst_ref=dst, send_sem=ssem.at[i * COPIES + k],
            recv_sem=rsem.at[i * COPIES + k], device_id=to,
            device_id_type=pl.DeviceIdType.MESH)
        copies[i, k].start()

    def got(i, k, n=1):
        for j in range(n):
            copies[i, k + j].wait_recv()

    loads = [pltpu.make_async_copy(s, d, lsem.at[j])
             for j, (s, d) in enumerate(((wg_hbm, wg), (wu_hbm, wu), (wd_hbm, wd)))]
    for ld in loads:
        ld.start()
    barrier = pltpu.get_barrier_semaphore()
    for o in others:
        pl.semaphore_signal(barrier, inc=1, device_id=o, device_id_type=pl.DeviceIdType.MESH)
    for k, ref in enumerate((x_in, c_in)):
        v = ref[...].astype(F32)
        for i in range(CHUNKS):
            zsrc[i, k] = v[8 * i:8 * i + 8]
    pl.semaphore_wait(barrier, len(others))

    def zl_send(i):
        send(i, ZL, zsrc.at[i], zdst.at[i], dev(zl_=1 - zl))

    def ag1(i):
        got(i, ZL)
        for k in range(2):
            own, oth = zsrc[i, k], zdst[i, k]
            lo = jnp.where(zl == 0, own, oth)
            hi = jnp.where(zl == 0, oth, own)
            xc[i, k, y, xx] = jnp.concatenate([lo, hi], axis=0).astype(BF16)
        for j in (1, 2, 3):
            blk = xc.at[i, 0, y, xx]
            send(i, X1 + j - 1, blk, blk, dev(x_=(xx + j) % 4))
            blk = xc.at[i, 1, y, xx]
            send(i, C1 + j - 1, blk, blk, dev(y_=(y + j) % 4))

    def ag2(i):
        got(i, X1, 3)
        for j in (1, 2, 3):
            blk = xc.at[i, 0, y]
            send(i, X2 + j - 1, blk, blk, dev(y_=(y + j) % 4))
        got(i, C1, 3)
        for j in (1, 2, 3):
            blk = xc.at[i, 1, :, xx]
            send(i, C2 + j - 1, blk, blk, dev(x_=(xx + j) % 4))

    def mm(i):
        got(i, X2, 3)
        xs = xc[i, 0].reshape(T, W)
        csnd[i, 0] = nn(xs, wg[:, theirs])
        send(i, CORE, csnd.at[i, 0], crcv.at[i, 0], dev(a_=1 - a))
        csnd[i, 1] = nn(xs, wu[:, theirs])
        send(i, CORE + 1, csnd.at[i, 1], crcv.at[i, 1], dev(a_=1 - a))
        got(i, C2, 3)
        cs = xc[i, 1].reshape(T, W)
        csnd[i, 2] = nt(cs, wd[theirs, :])
        send(i, CORE + 2, csnd.at[i, 2], crcv.at[i, 2], dev(a_=1 - a))
        part[i, 0] = nn(xs, wg[:, mine]).reshape(4, PIECE, HALF)
        part[i, 1] = nn(xs, wu[:, mine]).reshape(4, PIECE, HALF)
        part[i, 2] = nt(cs, wd[mine, :]).reshape(4, PIECE, HALF)

    def rs1(i):
        got(i, CORE, 3)
        for j in range(3):
            part[i, j] = part[i, j] + crcv[i, j].reshape(4, PIECE, HALF)
        zsnd[i, 0] = part[i, :, opp].astype(BF16)
        send(i, ZA, zsnd.at[i, 0], zrcv.at[i, 0], dev(zh_=nxt))
        zsnd[i, 1] = part[i, :, prv].astype(BF16)
        send(i, ZB, zsnd.at[i, 1], zrcv.at[i, 1], dev(zh_=prv))

    def rs2(i):
        got(i, ZA)
        zsnd[i, 2] = (part[i, :, nxt] + zrcv[i, 0].astype(F32)).astype(BF16)
        send(i, ZC, zsnd.at[i, 2], zrcv.at[i, 2], dev(zh_=nxt))

    def el(i):
        got(i, ZB)
        got(i, ZC)
        tot = part[i, :, zh] + zrcv[i, 1].astype(F32) + zrcv[i, 2].astype(F32)
        gate, up, slope = tot[0], tot[1], tot[2]
        sig = 1.0 / (1.0 + jnp.exp(-gate))
        act = gate * sig
        hid[i, 0, zh, :, mine] = (act * up).astype(BF16)
        hid[i, 1, zh, :, mine] = (slope * up * sig * (1.0 + gate * (1.0 - sig))).astype(BF16)
        hid[i, 2, zh, :, mine] = (slope * act).astype(BF16)
        blk = hid.at[i, :, zh, :, mine]
        send(i, GN, blk, blk, dev(zh_=nxt))
        send(i, GP, blk, blk, dev(zh_=prv))
        send(i, GC, blk, blk, dev(a_=1 - a))

    def fw(i):
        got(i, GN)
        blk = hid.at[i, :, prv, :, mine]
        send(i, GF, blk, blk, dev(zh_=nxt))
        send(i, GC + 1, blk, blk, dev(a_=1 - a))
        got(i, GP)
        blk = hid.at[i, :, nxt, :, mine]
        send(i, GC + 2, blk, blk, dev(a_=1 - a))

    def fw2(i):
        got(i, GF)
        blk = hid.at[i, :, opp, :, mine]
        send(i, GC + 3, blk, blk, dev(a_=1 - a))

    def out(i):
        got(i, GC, 4)
        h = [hid[i, j].reshape(T, W) for j in range(3)]

        def cols_out(n, _):
            ds = pl.ds(pl.multiple_of(n * 256, 256), 256)
            p = nn(h[0], wd[:, ds]).reshape(4, 4, ROWS, 256)
            pf[0, :, :, :, ds] = p
            psnd[i, 0, :, :, :, ds] = p.astype(BF16)
            return _

        def cols_gt(n, _):
            ds = pl.ds(pl.multiple_of(n * 256, 256), 256)
            p = (nt(h[1], wg[ds, :]) + nt(h[2], wu[ds, :])).reshape(4, 4, ROWS, 256)
            pf[1, :, :, :, ds] = p
            psnd[i, 1, :, :, :, ds] = p.astype(BF16)
            return _

        lax.fori_loop(0, 3, cols_out, 0)
        for j in (1, 2, 3):
            to = (xx + j) % 4
            send(i, O1 + j - 1, psnd.at[i, 0, :, to], p1rcv.at[i, 0, j - 1], dev(x_=to))
        lax.fori_loop(0, 3, cols_gt, 0)
        for j in (1, 2, 3):
            to = (y + j) % 4
            send(i, G1 + j - 1, psnd.at[i, 1, to], p1rcv.at[i, 1, j - 1], dev(y_=to))
        pown[i, 0] = pf[0, :, xx]
        pown[i, 1] = pf[1, y]

    def o2(i):
        for k, (first, second) in enumerate(((O1, O2), (G1, G2))):
            got(i, first, 3)
            t = pown[i, k]
            for j in range(3):
                t = t + p1rcv[i, k, j].astype(F32)
            sf[...] = t
            s1snd[i, k] = t.astype(BF16)
            for j in (1, 2, 3):
                if k == 0:
                    to = (y + j) % 4
                    where = dev(y_=to)
                else:
                    to = (xx + j) % 4
                    where = dev(x_=to)
                send(i, second + j - 1, s1snd.at[i, k, to], p2rcv.at[i, k, j - 1], where)
            s1own[i, k] = sf[y] if k == 0 else sf[xx]

    def o3(i):
        for k, second in enumerate((O2, G2)):
            got(i, second, 3)
            t = s1own[i, k]
            for j in range(3):
                t = t + p2rcv[i, k, j].astype(F32)
            fin[i, k] = t.reshape(2, 8, W)
        send(i, FIN, fin.at[i, :, 1 - zl], frcv.at[i], dev(zl_=1 - zl))

    def o4(i):
        got(i, FIN)
        for k in range(2):
            res[k, 8 * i:8 * i + 8] = fin[i, k, zl] + frcv[i, k]

    scale = W ** -0.5
    stores = []

    def grad(which):
        src, k, hbm = ((0, 1, gg_hbm), (0, 2, gu_hbm), (1, 0, gd_hbm))[which]

        def rows(n, _):
            ds = pl.ds(pl.multiple_of(n * 256, 256), 256)
            if which < 2:
                lhs = xc[:, 0, :, :, :, ds].reshape(W, 256)
                rhs = hid[:, k].reshape(W, W)
            else:
                lhs = hid[:, 0, :, :, ds].reshape(W, 256)
                rhs = xc[:, 1].reshape(W, W)
            grads[which, ds, :] = (tn(lhs, rhs) * scale).astype(BF16)
            return _

        lax.fori_loop(0, 3, rows, 0)
        st = pltpu.make_async_copy(grads.at[which], hbm, gsem.at[which])
        st.start()
        stores.append(st)

    for i in range(CHUNKS):
        zl_send(i)
    ag1(0)
    ag2(0)
    ag1(1)
    for ld in loads:
        ld.wait()
    mm(0)
    rs1(0)
    ag2(1)
    ag1(2)
    rs2(0)
    mm(1)
    rs1(1)
    ag2(2)
    el(0)
    rs2(1)
    mm(2)
    rs1(2)
    fw(0)
    el(1)
    rs2(2)
    fw2(0)
    out(0)
    fw(1)
    el(2)
    o2(0)
    fw2(1)
    o3(0)
    out(1)
    fw(2)
    o4(0)
    o2(1)
    fw2(2)
    o3(1)
    out(2)
    grad(0)
    o4(1)
    grad(1)
    o2(2)
    grad(2)
    o3(2)
    o4(2)
    out_ref[...] = res[0].astype(BF16)
    gt_ref[...] = res[1].astype(BF16)
    for c in copies.values():
        c.wait_send()
    for st in stores:
        st.wait()


def local(tokens, cotangent, gate_weight, up_weight, down_weight):
    vmem = pl.BlockSpec(memory_space=pltpu.VMEM)
    hbm = pl.BlockSpec(memory_space=pl.ANY)
    small = jax.ShapeDtypeStruct((LOCAL, W), BF16)
    big = jax.ShapeDtypeStruct((W, W), BF16)
    return pl.pallas_call(
        kernel,
        name="swiglu",
        out_shape=(small, small, big, big, big),
        in_specs=[vmem, vmem, hbm, hbm, hbm],
        out_specs=(vmem, vmem, hbm, hbm, hbm),
        scratch_shapes=[
            pltpu.VMEM((W, W), BF16),
            pltpu.VMEM((W, W), BF16),
            pltpu.VMEM((W, W), BF16),
            pltpu.VMEM((CHUNKS, 2, 8, W), F32),
            pltpu.VMEM((CHUNKS, 2, 8, W), F32),
            pltpu.VMEM((CHUNKS, 2, 4, 4, ROWS, W), BF16),
            pltpu.VMEM((CHUNKS, 3, T, HALF), F32),
            pltpu.VMEM((CHUNKS, 3, T, HALF), F32),
            pltpu.VMEM((CHUNKS, 3, 4, PIECE, HALF), F32),
            pltpu.VMEM((CHUNKS, 3, 3, PIECE, HALF), BF16),
            pltpu.VMEM((CHUNKS, 3, 3, PIECE, HALF), BF16),
            pltpu.VMEM((CHUNKS, 3, 4, PIECE, W), BF16),
            pltpu.VMEM((2, 4, 4, ROWS, W), F32),
            pltpu.VMEM((CHUNKS, 2, 4, 4, ROWS, W), BF16),
            pltpu.VMEM((CHUNKS, 2, 4, ROWS, W), F32),
            pltpu.VMEM((CHUNKS, 2, 3, 4, ROWS, W), BF16),
            pltpu.VMEM((4, ROWS, W), F32),
            pltpu.VMEM((CHUNKS, 2, 4, ROWS, W), BF16),
            pltpu.VMEM((CHUNKS, 2, ROWS, W), F32),
            pltpu.VMEM((CHUNKS, 2, 3, ROWS, W), BF16),
            pltpu.VMEM((CHUNKS, 2, 2, 8, W), F32),
            pltpu.VMEM((CHUNKS, 2, 8, W), F32),
            pltpu.VMEM((2, LOCAL, W), F32),
            pltpu.VMEM((3, W, W), BF16),
            pltpu.SemaphoreType.DMA((CHUNKS * COPIES,)),
            pltpu.SemaphoreType.DMA((CHUNKS * COPIES,)),
            pltpu.SemaphoreType.DMA((3,)),
            pltpu.SemaphoreType.DMA((3,)),
        ],
        compiler_params=pltpu.CompilerParams(
            collective_id=0, has_side_effects=True, vmem_limit_bytes=60 << 20),
        cost_estimate=pl.CostEstimate(
            flops=18 * W ** 3, bytes_accessed=12 * W * W, transcendentals=W * W // 8),
    )(tokens, cotangent, gate_weight, up_weight, down_weight)


def solution(mesh):
    by_token = P(("depth", "col"), "row")
    by_model = P("row", ("depth", "col"))
    return jax.shard_map(
        local,
        mesh=mesh,
        in_specs=(by_token, by_token, by_model, by_model, by_token),
        out_specs=(by_token, by_token, by_model, by_model, by_token),
        check_vma=False,
    )
```

time: 843 us -> 126 us (0.15)
  waiting for transfers between devices: 790 us -> 0 us
  Pallas kernels: 0 us -> 117 us
  matrix products: 26.8 us -> 0 us
  between operations: 13.9 us -> 0.64 us
    reduce_scatter x2 -> x0, waiting for transfers between devices: 314 us -> none  [the longest x1 164 us: local(): lax.psum_scatter(first_part + second_part, ('depth', 'col'), scatter_dime...]
    all_gather x2 -> x0, waiting for transfers between devices: 307 us -> none  [the longest x1 157 us: local(): shard_rows = lax.all_gather(tokens, ('depth', 'col'), axis=0, tiled=True)]
    psum x1 -> x0, waiting for transfers between devices: 168 us -> none  [local(): gate_value, up_value = lax.psum((gate_part, up_part), 'row')]
    pallas_call x0 -> x1, Pallas kernels: none -> 117 us  [local(): pl.pallas_call(kernel, name='swiglu', out_shape=(small, small, big, big,...]
    dot_general x9 -> x0, matrix products: 26.8 us -> none  [the longest x1 4.28 us: local(): up_part = jnp.dot(shard_rows, up_weight, preferred_element_type=jnp.float32)]
  transfers between devices with their start and end apart: 5 -> 0, of which waited for: 5 -> 0; matrix products, arithmetic and copies ran while one was open for 3% -> 0% of each run, Pallas kernels for 0% -> 0%
where the time goes in v1:
time: 126 us
  Pallas kernels  117 us (93%)
  local copies, waits for them, and re-layouts  7.94 us (6%)
    pallas_call x1, Pallas kernels, local(): pl.pallas_call(kernel, name='swiglu', out_shape=(small, small, big, big,...  117 us
    unnamed x9, local copies, waits for them, and re-layouts  7.94 us

profile of v1, /device:TPU:32, one launch (start us, length us, event | category | flops | bytes accessed | tf_op | source)
XLA Modules:
  0.0 125.7 jit_solution(4063058772861415322)
XLA Ops:
  0.6 117.1 %swiglu.1 = (bf16[24,768]{1,0:T(8,128)(2,1)}, bf16[24,768]{1,0:T(8,128)(2,1)}, bf16[768,768]{1,0:T(8,128)(2,1)}, bf16[768,768]{1,0:T(8,128)(2,1)}, bf16[768,768]{1,0:T(8,128)(2,1)}) custom-call(bf16[24,768]{1,0:T(8,128)(2,1)} %x_in.1, bf16[24,768]{1,0:T(8,128)(2,1)} %c_in.1, bf16[768,768]{1,0:T(8,128)(2,1)} %wg_hbm.1, bf16[768,768]{1,0:T(8,128)(2,1)} %wu_hbm.1, ...), custom_call_target="tpu_custom_call" | custom-call | flops 8153726976 | bytes 7077888 | tf_op jit(solution)/shard_map/swiglu/pallas_call | solution.py:303
  117.7 1.4 %copy.15 = bf16[24,768]{1,0:T(8,128)(2,1)} copy(bf16[24,768]{1,0:T(8,128)(2,1)} %get-tuple-element.10) | data formatting | bytes 73728
  119.1 1.4 %copy.16 = bf16[24,768]{1,0:T(8,128)(2,1)} copy(bf16[24,768]{1,0:T(8,128)(2,1)} %get-tuple-element.11) | data formatting | bytes 73728
  120.5 0.0 copy-start.1
  120.5 2.5 %copy.17 = bf16[768,768]{1,0:T(8,128)(2,1)} copy(bf16[768,768]{1,0:T(8,128)(2,1)} %get-tuple-element.12) | data formatting | bytes 2359296
  123.0 0.0 copy-done.1
  123.0 0.0 copy-start
  123.0 1.0 copy.18
  124.0 0.7 copy-done
  124.7 1.0 copy.19
Async XLA Ops:
  120.5 2.5 %copy-start.1 = (bf16[768,768]{1,0:T(8,128)(2,1)S(1)}, bf16[768,768]{1,0:T(8,128)(2,1)}, u32[]{:S(2)}) copy-start(bf16[768,768]{1,0:T(8,128)(2,1)} %get-tuple-element.13) | copy-start | bytes 3538948
  123.0 1.7 %copy-start = (bf16[768,768]{1,0:T(8,128)(2,1)S(1)}, bf16[768,768]{1,0:T(8,128)(2,1)}, u32[]{:S(2)}) copy-start(bf16[768,768]{1,0:T(8,128)(2,1)} %get-tuple-element.14) | copy-start | bytes 3538948

commit v2 on v1

v2 whole, which is shorter than its diff:
```python
import functools

import jax
import jax.numpy as jnp
from jax import lax
from jax.experimental import pallas as pl
from jax.experimental.pallas import tpu as pltpu
from jax.sharding import PartitionSpec as P

F32 = jnp.float32
BF16 = jnp.bfloat16
W = 768
HALF = W // 2
LOCAL = 24
UNIT = 128

SIZES = (1, 1, 2, 1, 1)
OWN = (0, 4, 5)
OTHER = (1, 2, 3)

X1, C1, X2, C2, CORE, ZA, ZB, ZC, GN, GP, GF, GC, O1, G1, O2, G2 = (
    0, 3, 6, 9, 12, 15, 16, 17, 18, 19, 20, 21, 25, 28, 31, 34)
COPIES = 37
ZL, FIN = 0, 3
SEMS = COPIES * len(SIZES) + 4

PLAN = (
    ("zl_send", 0), ("zl_send", 1), ("zl_send", 2), ("ready", 0), ("ag1", 0), ("ag1", 1),
    ("ag2", 0), ("ag1", 2), ("ag1", 3), ("ag1", 4), ("ag2", 1), ("mm", 0),
    ("ag2", 2), ("ag2", 3), ("ag2", 4), ("rs1", 0), ("mm", 1), ("rs2", 0),
    ("rs1", 1), ("mm", 2), ("el", 0), ("mm", 3), ("rs2", 1), ("mm", 4),
    ("fw", 0), ("rs1", 2), ("fp", 0), ("el", 1), ("fw2", 0), ("out", 0),
    ("rs2", 2), ("o2", 0), ("o3", 0), ("sent", 0), ("fw", 1), ("rs1", 3),
    ("fp", 1), ("el", 2), ("fw2", 1), ("out", 1), ("rs2", 3), ("o2", 1),
    ("fw", 2), ("rs1", 4), ("o3", 1), ("sent", 1), ("fp", 2), ("el", 3),
    ("fw2", 2), ("out", 2), ("rs2", 4), ("fw", 3), ("fp", 3), ("el", 4),
    ("o2", 2), ("fw2", 3), ("out", 3), ("fw", 4), ("o3", 2), ("sent", 2),
    ("fp", 4), ("o2", 3), ("fw2", 4), ("fin_send", 0), ("out", 4), ("o3", 3),
    ("grad", 0), ("grad", 1), ("grad", 2), ("o2", 4), ("sent", 3), ("o3", 4),
    ("sent", 4), ("end", 0),
)


def nt(a, b):
    return lax.dot_general(a, b, (((1,), (1,)), ((), ())), preferred_element_type=F32)


def nn(a, b):
    return jnp.dot(a, b, preferred_element_type=F32)


def tn(a, b):
    return lax.dot_general(a, b, (((0,), (0,)), ((), ())), preferred_element_type=F32)


def fold(v):
    v = v.reshape(v.shape[0] // 8, 8, W)
    return jnp.concatenate([v[:, :, :HALF], v[:, :, HALF:]], axis=1)


def unfold(v):
    v = jnp.concatenate([v[:, :8], v[:, 8:]], axis=2)
    return v.reshape(v.shape[0] * 8, W)


def kernel(plan, x_in, c_in, wg_hbm, wu_hbm, wd_hbm,
           out_ref, gt_ref, gg_hbm, gu_hbm, gd_hbm,
           wg, wu, wd, xc, xg, csnd, crcv, part, zsnd, zrcv, hid,
           pf, psnd, p1rcv, sf, s1snd, s1own, p2rcv, fin, frcv,
           grads, ssem, rsem, lsem, gsem):
    depth, row, xx = lax.axis_index("depth"), lax.axis_index("row"), lax.axis_index("col")
    zl, y, zh, a = depth // 4, depth % 4, row // 2, row % 2
    nxt, prv, opp = (zh + 1 + 2 * a) % 4, (zh + 3 + 2 * a) % 4, (zh + 2) % 4

    def dev(zl_=zl, y_=y, zh_=zh, a_=a, x_=xx):
        return (zl_ * 4 + y_, zh_ * 2 + a_, x_)

    others = ([dev(zl_=1 - zl), dev(a_=1 - a), dev(zh_=nxt), dev(zh_=prv)]
              + [dev(x_=(xx + j) % 4) for j in (1, 2, 3)]
              + [dev(y_=(y + j) % 4) for j in (1, 2, 3)])
    mine = pl.ds(pl.multiple_of(a * HALF, 128), HALF)
    theirs = pl.ds(pl.multiple_of((1 - a) * HALF, 128), HALF)
    copies = {}

    def units(i):
        return slice(sum(SIZES[:i]), sum(SIZES[:i + 1]))

    def rows(i):
        return slice(UNIT * sum(SIZES[:i]), UNIT * sum(SIZES[:i + 1]))

    def quarter(i):
        return slice(UNIT // 4 * sum(SIZES[:i]), UNIT // 4 * sum(SIZES[:i + 1]))

    def piece(i, q):
        n = UNIT // 4 * SIZES[i]
        return pl.ds(pl.multiple_of(UNIT * sum(SIZES[:i]) + n * q, 32), n)

    def send(i, k, src, dst, to):
        s = COPIES * i + k
        copies[i, k] = pltpu.make_async_remote_copy(
            src_ref=src, dst_ref=dst, send_sem=ssem.at[s], recv_sem=rsem.at[s],
            device_id=to, device_id_type=pl.DeviceIdType.MESH)
        copies[i, k].start()

    def got(i, k, n=1):
        for j in range(n):
            copies[i, k + j].wait_recv()

    glob = len(SIZES)

    loads = [pltpu.make_async_copy(s, d, lsem.at[j])
             for j, (s, d) in enumerate(((wg_hbm, wg), (wu_hbm, wu), (wd_hbm, wd)))]
    for ld in loads:
        ld.start()
    barrier = pltpu.get_barrier_semaphore()
    for o in others:
        pl.semaphore_signal(barrier, inc=1, device_id=o, device_id_type=pl.DeviceIdType.MESH)
    for k, ref in enumerate((x_in, c_in)):
        v = fold(ref[...].astype(F32)).astype(BF16)
        for u in range(3):
            xc[k, OWN[u], y, xx] = v[u]
    pl.semaphore_wait(barrier, len(others))

    def zl_send(u):
        send(glob, ZL + u, xc.at[:, OWN[u], y, xx], xc.at[:, OTHER[u], y, xx], dev(zl_=1 - zl))

    def ag1(i):
        es = units(i)
        for e in range(es.start, es.stop):
            if e in OTHER:
                got(glob, ZL + OTHER.index(e))
        for j in (1, 2, 3):
            blk = xc.at[0, es, y, xx]
            send(i, X1 + j - 1, blk, blk, dev(x_=(xx + j) % 4))
            blk = xc.at[1, es, y, xx]
            send(i, C1 + j - 1, blk, blk, dev(y_=(y + j) % 4))

    def ag2(i):
        es = units(i)
        got(i, X1, 3)
        for j in (1, 2, 3):
            blk = xc.at[0, es, y]
            send(i, X2 + j - 1, blk, blk, dev(y_=(y + j) % 4))
        got(i, C1, 3)
        for j in (1, 2, 3):
            blk = xc.at[1, es, :, xx]
            send(i, C2 + j - 1, blk, blk, dev(x_=(xx + j) % 4))

    def ready(_):
        for ld in loads:
            ld.wait()

    def gathered(i, k):
        v = xc[k, units(i)].reshape(16 * SIZES[i], 16, HALF)
        v = unfold(v.astype(F32)).astype(BF16)
        xg[k, rows(i)] = v
        return v

    def mm(i):
        rs = rows(i)
        got(i, X2, 3)
        xs = gathered(i, 0)
        csnd[0, rs] = nn(xs, wg[:, theirs])
        send(i, CORE, csnd.at[0, rs], crcv.at[0, rs], dev(a_=1 - a))
        csnd[1, rs] = nn(xs, wu[:, theirs])
        send(i, CORE + 1, csnd.at[1, rs], crcv.at[1, rs], dev(a_=1 - a))
        got(i, C2, 3)
        cs = gathered(i, 1)
        csnd[2, rs] = nt(cs, wd[theirs, :])
        send(i, CORE + 2, csnd.at[2, rs], crcv.at[2, rs], dev(a_=1 - a))
        part[0, rs] = nn(xs, wg[:, mine])
        part[1, rs] = nn(xs, wu[:, mine])
        part[2, rs] = nt(cs, wd[mine, :])

    def rs1(i):
        rs, qs = rows(i), quarter(i)
        got(i, CORE, 3)
        part[:, rs] = part[:, rs] + crcv[:, rs]
        zsnd[0, :, qs] = part[:, piece(i, opp)].astype(BF16)
        send(i, ZA, zsnd.at[0, :, qs], zrcv.at[0, :, qs], dev(zh_=nxt))
        zsnd[1, :, qs] = part[:, piece(i, prv)].astype(BF16)
        send(i, ZB, zsnd.at[1, :, qs], zrcv.at[1, :, qs], dev(zh_=prv))

    def rs2(i):
        qs = quarter(i)
        got(i, ZA)
        zsnd[2, :, qs] = (part[:, piece(i, nxt)] + zrcv[0, :, qs].astype(F32)).astype(BF16)
        send(i, ZC, zsnd.at[2, :, qs], zrcv.at[2, :, qs], dev(zh_=nxt))

    def el(i):
        qs, ps = quarter(i), piece(i, zh)
        got(i, ZB)
        got(i, ZC)
        tot = part[:, ps] + zrcv[1, :, qs].astype(F32) + zrcv[2, :, qs].astype(F32)
        gate, up, slope = tot[0], tot[1], tot[2]
        sig = 1.0 / (1.0 + jnp.exp(-gate))
        act = gate * sig
        hid[0, ps, mine] = (act * up).astype(BF16)
        hid[1, ps, mine] = (slope * up * sig * (1.0 + gate * (1.0 - sig))).astype(BF16)
        hid[2, ps, mine] = (slope * act).astype(BF16)
        blk = hid.at[:, ps, mine]
        send(i, GN, blk, blk, dev(zh_=nxt))
        send(i, GP, blk, blk, dev(zh_=prv))
        send(i, GC, blk, blk, dev(a_=1 - a))

    def fw(i):
        got(i, GN)
        blk = hid.at[:, piece(i, prv), mine]
        send(i, GF, blk, blk, dev(zh_=nxt))
        send(i, GC + 1, blk, blk, dev(a_=1 - a))

    def fp(i):
        got(i, GP)
        blk = hid.at[:, piece(i, nxt), mine]
        send(i, GC + 2, blk, blk, dev(a_=1 - a))

    def fw2(i):
        got(i, GF)
        blk = hid.at[:, piece(i, opp), mine]
        send(i, GC + 3, blk, blk, dev(a_=1 - a))

    def out(i):
        rs, es, n = rows(i), units(i), SIZES[i]
        got(i, GC, 4)
        p = fold(nn(hid[0, rs], wd[...])).reshape(n, 4, 4, 16, HALF)
        pf[0, es] = p
        psnd[0, es] = p.astype(BF16)
        for j in (1, 2, 3):
            to = (xx + j) % 4
            send(i, O1 + j - 1, psnd.at[0, es, :, to], p1rcv.at[0, j - 1, es], dev(x_=to))
        p = fold(nt(hid[1, rs], wg[...]) + nt(hid[2, rs], wu[...])).reshape(n, 4, 4, 16, HALF)
        pf[1, es] = p
        psnd[1, es] = p.astype(BF16)
        for j in (1, 2, 3):
            to = (y + j) % 4
            send(i, G1 + j - 1, psnd.at[1, es, to], p1rcv.at[1, j - 1, es], dev(y_=to))

    def o2(i):
        es = units(i)
        for k, (first, second) in enumerate(((O1, O2), (G1, G2))):
            got(i, first, 3)
            t = pf[0, es, :, xx] if k == 0 else pf[1, es, y]
            for j in range(3):
                t = t + p1rcv[k, j, es].astype(F32)
            sf[:SIZES[i]] = t
            s1snd[k, es] = t.astype(BF16)
            for j in (1, 2, 3):
                if k == 0:
                    to = (y + j) % 4
                    where = dev(y_=to)
                else:
                    to = (xx + j) % 4
                    where = dev(x_=to)
                send(i, second + j - 1, s1snd.at[k, es, to], p2rcv.at[k, j - 1, es], where)
            s1own[k, es] = sf[:SIZES[i], y] if k == 0 else sf[:SIZES[i], xx]

    def o3(i):
        es = units(i)
        for k, second in enumerate((O2, G2)):
            got(i, second, 3)
            t = s1own[k, es]
            for j in range(3):
                t = t + p2rcv[k, j, es].astype(F32)
            fin[k, es] = t

    def fin_send(_):
        send(glob, FIN, fin.at[:, OTHER[0]:OTHER[-1] + 1], frcv, dev(zl_=1 - zl))

    def sent(i):
        for k in range(COPIES):
            copies[i, k].wait_send()

    scale = W ** -0.5
    stores = []

    def grad(which):
        lhs, k, hbm = ((xg.at[0], 1, gg_hbm), (xg.at[0], 2, gu_hbm), (hid.at[0], 0, gd_hbm))[which]

        def tile(n, _):
            ds = pl.ds(pl.multiple_of(n * 256, 256), 256)
            rhs = hid[k] if which < 2 else xg[1]
            grads[which, ds, :] = (tn(lhs[:, ds], rhs) * scale).astype(BF16)
            return _

        lax.fori_loop(0, 3, tile, 0)
        st = pltpu.make_async_copy(grads.at[which], hbm, gsem.at[which])
        st.start()
        stores.append(st)

    def end(_):
        got(glob, FIN)
        for k, ref in enumerate((out_ref, gt_ref)):
            v = jnp.stack([fin[k, e] for e in OWN]) + frcv[k]
            ref[...] = unfold(v).astype(BF16)

    steps = {f.__name__: f for f in (zl_send, ag1, ag2, ready, mm, rs1, rs2, el, fw, fp, fw2,
                                     out, o2, o3, fin_send, sent, grad, end)}
    for name, i in plan:
        steps[name](i)
    for st in stores:
        st.wait()
    for k in (ZL, ZL + 1, ZL + 2, FIN):
        copies[glob, k].wait_send()


def move(a, b, c, d, e, a_out, b_out, c_out, d_out, e_out, sem):
    pairs = ((c, c_out), (d, d_out), (e, e_out), (a, a_out), (b, b_out))
    moves = [pltpu.make_async_copy(s, t, sem.at[j]) for j, (s, t) in enumerate(pairs)]
    for m in moves:
        m.start()
    for m in moves:
        m.wait()


def local(tokens, cotangent, gate_weight, up_weight, down_weight):
    vmem = pl.BlockSpec(memory_space=pltpu.VMEM)
    hbm = pl.BlockSpec(memory_space=pl.ANY)
    small = jax.ShapeDtypeStruct((LOCAL, W), BF16)
    big = jax.ShapeDtypeStruct((W, W), BF16)
    results = pl.pallas_call(
        functools.partial(kernel, PLAN),
        name="swiglu",
        out_shape=(small, small, big, big, big),
        in_specs=[vmem, vmem, hbm, hbm, hbm],
        out_specs=(vmem, vmem, hbm, hbm, hbm),
        scratch_shapes=[
            pltpu.VMEM((W, W), BF16),
            pltpu.VMEM((W, W), BF16),
            pltpu.VMEM((W, W), BF16),
            pltpu.VMEM((2, 6, 4, 4, 16, HALF), BF16),
            pltpu.VMEM((2, W, W), BF16),
            pltpu.VMEM((3, W, HALF), F32),
            pltpu.VMEM((3, W, HALF), F32),
            pltpu.VMEM((3, W, HALF), F32),
            pltpu.VMEM((3, 3, W // 4, HALF), BF16),
            pltpu.VMEM((3, 3, W // 4, HALF), BF16),
            pltpu.VMEM((3, W, W), BF16),
            pltpu.VMEM((2, 6, 4, 4, 16, HALF), F32),
            pltpu.VMEM((2, 6, 4, 4, 16, HALF), BF16),
            pltpu.VMEM((2, 3, 6, 4, 16, HALF), BF16),
            pltpu.VMEM((max(SIZES), 4, 16, HALF), F32),
            pltpu.VMEM((2, 6, 4, 16, HALF), BF16),
            pltpu.VMEM((2, 6, 16, HALF), F32),
            pltpu.VMEM((2, 3, 6, 16, HALF), BF16),
            pltpu.VMEM((2, 6, 16, HALF), F32),
            pltpu.VMEM((2, 3, 16, HALF), F32),
            pltpu.VMEM((3, W, W), BF16),
            pltpu.SemaphoreType.DMA((SEMS,)),
            pltpu.SemaphoreType.DMA((SEMS,)),
            pltpu.SemaphoreType.DMA((3,)),
            pltpu.SemaphoreType.DMA((3,)),
        ],
        compiler_params=pltpu.CompilerParams(
            collective_id=0, has_side_effects=True, vmem_limit_bytes=56 << 20),
        cost_estimate=pl.CostEstimate(
            flops=18 * W ** 3, bytes_accessed=12 * W * W, transcendentals=W * W // 8),
    )(tokens, cotangent, gate_weight, up_weight, down_weight)
    return pl.pallas_call(
        move,
        name="move",
        out_shape=(small, small, big, big, big),
        in_specs=[hbm] * 5,
        out_specs=(hbm,) * 5,
        scratch_shapes=[pltpu.SemaphoreType.DMA((5,))],
    )(*results)


def solution(mesh):
    by_token = P(("depth", "col"), "row")
    by_model = P("row", ("depth", "col"))
    return jax.shard_map(
        local,
        mesh=mesh,
        in_specs=(by_token, by_token, by_model, by_model, by_token),
        out_specs=(by_token, by_token, by_model, by_model, by_token),
        check_vma=False,
    )
```

time: 126 us -> 228 us (1.81)
  the two profiles are of different devices: /device:TPU:32 before, /device:TPU:1 now
where the time goes in v2:
time: 228 us
  Pallas kernels  227 us (100%)
    pallas_call x1, Pallas kernels, local(): pl.pallas_call(functools.partial(kernel, PLAN), name='swiglu', out_shape=...  117 us
    pallas_call x1, Pallas kernels, local(): pl.pallas_call(move, name='move', out_shape=(small, small, big, big, big)...  111 us

profile of v2, /device:TPU:1, one launch (start us, length us, event | category | flops | bytes accessed | tf_op | source)
XLA Modules:
  0.0 228.1 jit_solution(1599676208613538729)
XLA Ops:
  0.6 116.7 %swiglu.1 = (bf16[24,768]{1,0:T(8,128)(2,1)}, bf16[24,768]{1,0:T(8,128)(2,1)}, bf16[768,768]{1,0:T(8,128)(2,1)}, bf16[768,768]{1,0:T(8,128)(2,1)}, bf16[768,768]{1,0:T(8,128)(2,1)}) custom-call(bf16[24,768]{1,0:T(8,128)(2,1)} %x_in.1, bf16[24,768]{1,0:T(8,128)(2,1)} %c_in.1, bf16[768,768]{1,0:T(8,128)(2,1)} %wg_hbm.1, bf16[768,768]{1,0:T(8,128)(2,1)} %wu_hbm.1, ...), custom_call_target="tpu_custom_call" | custom-call | flops 8153726976 | bytes 7077888 | tf_op jit(solution)/shard_map/swiglu/pallas_call | solution.py:320
  117.3 110.6 %move.1 = (bf16[24,768]{1,0:T(8,128)(2,1)}, bf16[24,768]{1,0:T(8,128)(2,1)}, bf16[768,768]{1,0:T(8,128)(2,1)}, bf16[768,768]{1,0:T(8,128)(2,1)}, bf16[768,768]{1,0:T(8,128)(2,1)}) custom-call(bf16[24,768]{1,0:T(8,128)(2,1)} %get-tuple-element.10.a, bf16[24,768]{1,0:T(8,128)(2,1)} %get-tuple-element.11.b, bf16[768,768]{1,0:T(8,128)(2,1)} %get-tuple-element.12.c, ...), custom_call_target="tpu_custom_call" | custom-call | tf_op jit(solution)/shard_map/move/pallas_call | solution.py:358

commit v3 on v2

v3 whole, which is shorter than its diff:
```python
import functools

import jax
import jax.numpy as jnp
from jax import lax
from jax.experimental import pallas as pl
from jax.experimental.pallas import tpu as pltpu
from jax.sharding import PartitionSpec as P

F32 = jnp.float32
BF16 = jnp.bfloat16
W = 768
HALF = W // 2
LOCAL = 24
UNIT = 128

SIZES = (1, 1, 2, 1, 1)
OWN = (0, 4, 5)
OTHER = (1, 2, 3)

X1, C1, X2, C2, CORE, ZA, ZB, ZC, GN, GP, GF, GC, O1, G1, O2, G2 = range(16)
KINDS = 16
ZL, FIN = 0, 3
SENDS = KINDS + 2
RECVS = KINDS * len(SIZES) + 4

PLAN = (
    ("ag1", 3), ("ag1", 0), ("ready", 0), ("ag1", 4), ("zl_send", 0), ("zl_send", 2),
    ("ag2c", 3), ("ag2x", 3), ("zl_send", 1), ("ag2x", 0), ("ag2c", 0), ("ag1", 1),
    ("mmc", 3), ("mmx", 3), ("mmx", 0), ("rs1", 3), ("ag1", 2), ("ag2x", 1),
    ("ag2c", 1), ("mmc", 0), ("rs1", 0), ("rs2", 3), ("ag2c", 4), ("mmc", 1),
    ("mmx", 1), ("ag2c", 2), ("ag2x", 2), ("rs2", 0), ("rs1", 1), ("el", 3),
    ("rs2", 1), ("el", 0), ("mmc", 2), ("ag2x", 4), ("mmx", 2), ("fw", 3),
    ("rs1", 2), ("fp", 3), ("fw2", 3), ("el", 1), ("outa", 3), ("fp", 0),
    ("mmc", 4), ("outb", 3), ("fw", 0), ("mmx", 4), ("rs2", 2), ("fp", 1),
    ("fw", 1), ("rs1", 4), ("fw2", 0), ("el", 2), ("fw2", 1), ("outa", 1),
    ("outa", 0), ("o2b", 3), ("rs2", 4), ("outb", 0), ("outb", 1), ("fw", 2),
    ("o2a", 1), ("el", 4), ("o3b", 3), ("fp", 2), ("fw2", 2), ("fw", 4),
    ("outa", 2), ("outb", 2), ("o2a", 0), ("o2b", 1), ("fp", 4), ("fw2", 4),
    ("outa", 4), ("o2a", 2), ("o3b", 1), ("o2a", 3), ("o2b", 2), ("outb", 4),
    ("grad", 2), ("o3a", 2), ("o2b", 0), ("o2a", 4), ("o3a", 1), ("o3b", 2),
    ("fin_send", 0), ("grad", 1), ("o2b", 4), ("grad", 0), ("o3b", 0), ("o3a", 3),
    ("o3a", 4), ("o3a", 0), ("o3b", 4), ("sent", 0), ("end", 0),
)


def nt(a, b):
    return lax.dot_general(a, b, (((1,), (1,)), ((), ())), preferred_element_type=F32)


def nn(a, b):
    return jnp.dot(a, b, preferred_element_type=F32)


def tn(a, b):
    return lax.dot_general(a, b, (((0,), (0,)), ((), ())), preferred_element_type=F32)


def fold(v):
    v = v.reshape(v.shape[0] // 8, 8, W)
    return jnp.concatenate([v[:, :, :HALF], v[:, :, HALF:]], axis=1)


def unfold(v):
    v = jnp.concatenate([v[:, :8], v[:, 8:]], axis=2)
    return v.reshape(v.shape[0] * 8, W)


def kernel(plan, x_in, c_in, wg_hbm, wu_hbm, wd_hbm,
           out_ref, gt_ref, gg_hbm, gu_hbm, gd_hbm,
           wg, wu, wd, xc, xg, csnd, crcv, part, zsnd, zrcv, hid,
           pf, psnd, p1rcv, sf, s1snd, s1own, p2rcv, fin, frcv,
           grads, ssem, rsem, lsem, gsem):
    depth, row, xx = lax.axis_index("depth"), lax.axis_index("row"), lax.axis_index("col")
    zl, y, zh, a = depth // 4, depth % 4, row // 2, row % 2
    nxt, prv, opp = (zh + 1 + 2 * a) % 4, (zh + 3 + 2 * a) % 4, (zh + 2) % 4

    def dev(zl_=zl, y_=y, zh_=zh, a_=a, x_=xx):
        return (zl_ * 4 + y_, zh_ * 2 + a_, x_)

    others = ([dev(zl_=1 - zl), dev(a_=1 - a), dev(zh_=nxt), dev(zh_=prv)]
              + [dev(x_=(xx + j) % 4) for j in (1, 2, 3)]
              + [dev(y_=(y + j) % 4) for j in (1, 2, 3)])
    mine = pl.ds(pl.multiple_of(a * HALF, 128), HALF)
    theirs = pl.ds(pl.multiple_of((1 - a) * HALF, 128), HALF)
    def units(i):
        return slice(sum(SIZES[:i]), sum(SIZES[:i + 1]))

    def rows(i):
        return slice(UNIT * sum(SIZES[:i]), UNIT * sum(SIZES[:i + 1]))

    def quarter(i):
        return slice(UNIT // 4 * sum(SIZES[:i]), UNIT // 4 * sum(SIZES[:i + 1]))

    def piece(i, q):
        n = UNIT // 4 * SIZES[i]
        return pl.ds(pl.multiple_of(UNIT * sum(SIZES[:i]) + n * q, 32), n)

    def push(ssem_at, rsem_at, src, dst, to):
        pltpu.make_async_remote_copy(
            src_ref=src, dst_ref=dst, send_sem=ssem.at[ssem_at], recv_sem=rsem.at[rsem_at],
            device_id=to, device_id_type=pl.DeviceIdType.MESH).start()

    def send(i, k, src, dst, to):
        push(k, KINDS * i + k, src, dst, to)

    def wait(sem, ref):
        pltpu.make_async_copy(ref, ref, sem).wait()

    def got(i, k, ref):
        wait(rsem.at[KINDS * i + k], ref)

    last = KINDS * len(SIZES)

    loads = [pltpu.make_async_copy(s, d, lsem.at[j])
             for j, (s, d) in enumerate(((wg_hbm, wg), (wu_hbm, wu), (wd_hbm, wd)))]
    for ld in loads:
        ld.start()
    barrier = pltpu.get_barrier_semaphore()
    for o in others:
        pl.semaphore_signal(barrier, inc=1, device_id=o, device_id_type=pl.DeviceIdType.MESH)
    for k, ref in enumerate((x_in, c_in)):
        v = fold(ref[...].astype(F32)).astype(BF16)
        for u in range(3):
            xc[k, OWN[u], y, xx] = v[u]
    pl.semaphore_wait(barrier, len(others))

    def zl_send(u):
        push(KINDS, last + ZL + u,
             xc.at[:, OWN[u], y, xx], xc.at[:, OTHER[u], y, xx], dev(zl_=1 - zl))

    def ag1(i):
        es = units(i)
        for e in range(es.start, es.stop):
            if e in OTHER:
                wait(rsem.at[last + ZL + OTHER.index(e)], xc.at[:, e, y, xx])
        for j in (1, 2, 3):
            blk = xc.at[0, es, y, xx]
            send(i, X1, blk, blk, dev(x_=(xx + j) % 4))
            blk = xc.at[1, es, y, xx]
            send(i, C1, blk, blk, dev(y_=(y + j) % 4))

    def ag2x(i):
        es = units(i)
        got(i, X1, xc.at[0, es, y, :3])
        for j in (1, 2, 3):
            blk = xc.at[0, es, y]
            send(i, X2, blk, blk, dev(y_=(y + j) % 4))

    def ag2c(i):
        es = units(i)
        got(i, C1, xc.at[1, es, :3, xx])
        for j in (1, 2, 3):
            blk = xc.at[1, es, :, xx]
            send(i, C2, blk, blk, dev(x_=(xx + j) % 4))

    def ready(_):
        for ld in loads:
            ld.wait()

    def gathered(i, k):
        v = xc[k, units(i)].reshape(16 * SIZES[i], 16, HALF)
        v = unfold(v.astype(F32)).astype(BF16)
        xg[k, rows(i)] = v
        return v

    def mmx(i):
        rs = rows(i)
        got(i, X2, xc.at[0, units(i), :3])
        xs = gathered(i, 0)
        for j, w in ((0, wg), (1, wu)):
            csnd[j, rs] = nn(xs, w[:, theirs])
            send(i, CORE, csnd.at[j, rs], crcv.at[j, rs], dev(a_=1 - a))
        part[0, rs] = nn(xs, wg[:, mine])
        part[1, rs] = nn(xs, wu[:, mine])

    def mmc(i):
        rs = rows(i)
        got(i, C2, xc.at[1, units(i), :3])
        cs = gathered(i, 1)
        csnd[2, rs] = nt(cs, wd[theirs, :])
        send(i, CORE, csnd.at[2, rs], crcv.at[2, rs], dev(a_=1 - a))
        part[2, rs] = nt(cs, wd[mine, :])

    def rs1(i):
        rs, qs = rows(i), quarter(i)
        got(i, CORE, crcv.at[:, rs])
        part[:, rs] = part[:, rs] + crcv[:, rs]
        zsnd[0, :, qs] = part[:, piece(i, opp)].astype(BF16)
        send(i, ZA, zsnd.at[0, :, qs], zrcv.at[0, :, qs], dev(zh_=nxt))
        zsnd[1, :, qs] = part[:, piece(i, prv)].astype(BF16)
        send(i, ZB, zsnd.at[1, :, qs], zrcv.at[1, :, qs], dev(zh_=prv))

    def rs2(i):
        qs = quarter(i)
        got(i, ZA, zrcv.at[0, :, qs])
        zsnd[2, :, qs] = (part[:, piece(i, nxt)] + zrcv[0, :, qs].astype(F32)).astype(BF16)
        send(i, ZC, zsnd.at[2, :, qs], zrcv.at[2, :, qs], dev(zh_=nxt))

    def el(i):
        qs, ps = quarter(i), piece(i, zh)
        got(i, ZB, zrcv.at[1, :, qs])
        got(i, ZC, zrcv.at[2, :, qs])
        tot = part[:, ps] + zrcv[1, :, qs].astype(F32) + zrcv[2, :, qs].astype(F32)
        gate, up, slope = tot[0], tot[1], tot[2]
        sig = 1.0 / (1.0 + jnp.exp(-gate))
        act = gate * sig
        hid[0, ps, mine] = (act * up).astype(BF16)
        hid[1, ps, mine] = (slope * up * sig * (1.0 + gate * (1.0 - sig))).astype(BF16)
        hid[2, ps, mine] = (slope * act).astype(BF16)
        blk = hid.at[:, ps, mine]
        send(i, GN, blk, blk, dev(zh_=nxt))
        send(i, GP, blk, blk, dev(zh_=prv))
        send(i, GC, blk, blk, dev(a_=1 - a))

    def fw(i):
        blk = hid.at[:, piece(i, prv), mine]
        got(i, GN, blk)
        send(i, GF, blk, blk, dev(zh_=nxt))
        send(i, GC, blk, blk, dev(a_=1 - a))

    def fp(i):
        blk = hid.at[:, piece(i, nxt), mine]
        got(i, GP, blk)
        send(i, GC, blk, blk, dev(a_=1 - a))

    def fw2(i):
        blk = hid.at[:, piece(i, opp), mine]
        got(i, GF, blk)
        send(i, GC, blk, blk, dev(a_=1 - a))

    def outa(i):
        rs, es, n = rows(i), units(i), SIZES[i]
        got(i, GC, hid.at[:, rs, theirs])
        p = fold(nn(hid[0, rs], wd[...])).reshape(n, 4, 4, 16, HALF)
        pf[0, es] = p
        psnd[0, es] = p.astype(BF16)
        for j in (1, 2, 3):
            to = (xx + j) % 4
            send(i, O1, psnd.at[0, es, :, to], p1rcv.at[0, j - 1, es], dev(x_=to))

    def outb(i):
        rs, es, n = rows(i), units(i), SIZES[i]
        p = fold(nt(hid[1, rs], wg[...]) + nt(hid[2, rs], wu[...])).reshape(n, 4, 4, 16, HALF)
        pf[1, es] = p
        psnd[1, es] = p.astype(BF16)
        for j in (1, 2, 3):
            to = (y + j) % 4
            send(i, G1, psnd.at[1, es, to], p1rcv.at[1, j - 1, es], dev(y_=to))

    def second(i, k, t):
        es = units(i)
        for j in range(3):
            t = t + p1rcv[k, j, es].astype(F32)
        sf[:SIZES[i]] = t
        s1snd[k, es] = t.astype(BF16)

    def o2a(i):
        es = units(i)
        got(i, O1, p1rcv.at[0, :, es])
        second(i, 0, pf[0, es, :, xx])
        for j in (1, 2, 3):
            to = (y + j) % 4
            send(i, O2, s1snd.at[0, es, to], p2rcv.at[0, j - 1, es], dev(y_=to))
        s1own[0, es] = sf[:SIZES[i], y]

    def o2b(i):
        es = units(i)
        got(i, G1, p1rcv.at[1, :, es])
        second(i, 1, pf[1, es, y])
        for j in (1, 2, 3):
            to = (xx + j) % 4
            send(i, G2, s1snd.at[1, es, to], p2rcv.at[1, j - 1, es], dev(x_=to))
        s1own[1, es] = sf[:SIZES[i], xx]

    def third(i, k, kind):
        es = units(i)
        got(i, kind, p2rcv.at[k, :, es])
        t = s1own[k, es]
        for j in range(3):
            t = t + p2rcv[k, j, es].astype(F32)
        fin[k, es] = t

    def o3a(i):
        third(i, 0, O2)

    def o3b(i):
        third(i, 1, G2)

    def fin_send(_):
        push(KINDS + 1, last + FIN, fin.at[:, OTHER[0]:OTHER[-1] + 1], frcv, dev(zl_=1 - zl))

    def sent(_):
        block, half = xc.at[0, :, 0, :3], hid.at[:, :, :HALF]
        for k, ref in ((X1, block), (C1, block), (X2, xc.at[0, :, :3]), (C2, xc.at[1, :, :3]),
                       (CORE, csnd), (ZA, zsnd.at[0]), (ZB, zsnd.at[1]), (ZC, zsnd.at[2]),
                       (GN, zsnd.at[0]), (GP, zsnd.at[1]), (GF, zsnd.at[2]), (GC, half),
                       (O1, p1rcv.at[0]), (G1, p1rcv.at[1]), (O2, p2rcv.at[0]),
                       (G2, p2rcv.at[1]), (KINDS, xc.at[:, :3, 0, 0]), (KINDS + 1, frcv)):
            wait(ssem.at[k], ref)

    scale = W ** -0.5
    stores = []

    def grad(which):
        lhs, k, hbm = ((xg.at[0], 1, gg_hbm), (xg.at[0], 2, gu_hbm), (hid.at[0], 0, gd_hbm))[which]

        def tile(n, _):
            ds = pl.ds(pl.multiple_of(n * 256, 256), 256)
            rhs = hid[k] if which < 2 else xg[1]
            grads[which, ds, :] = (tn(lhs[:, ds], rhs) * scale).astype(BF16)
            return _

        lax.fori_loop(0, 3, tile, 0)
        st = pltpu.make_async_copy(grads.at[which], hbm, gsem.at[which])
        st.start()
        stores.append(st)

    def end(_):
        wait(rsem.at[last + FIN], frcv)
        for k, ref in enumerate((out_ref, gt_ref)):
            v = jnp.stack([fin[k, e] for e in OWN]) + frcv[k]
            ref[...] = unfold(v).astype(BF16)

    steps = {f.__name__: f for f in (
        zl_send, ag1, ag2x, ag2c, ready, mmx, mmc, rs1, rs2, el, fw, fp, fw2, outa, outb,
        o2a, o2b, o3a, o3b, fin_send, sent, grad, end)}
    for name, i in plan:
        steps[name](i)
    for st in stores:
        st.wait()


def move(*refs):
    srcs, dsts, bufs, isem, osem = refs[:5], refs[5:10], refs[10:15], refs[15], refs[16]
    parts = []
    for j in (2, 3, 4):
        for q in range(4):
            ds = pl.ds(q * W // 4, W // 4)
            parts.append((srcs[j].at[ds], bufs[j].at[ds], dsts[j].at[ds]))
    for j in (0, 1):
        parts.append((srcs[j], bufs[j], dsts[j]))
    loads = [pltpu.make_async_copy(s, b, isem.at[n]) for n, (s, b, _) in enumerate(parts)]
    stores = [pltpu.make_async_copy(b, d, osem.at[n]) for n, (_, b, d) in enumerate(parts)]
    for ld in loads:
        ld.start()
    for ld, st in zip(loads, stores):
        ld.wait()
        st.start()
    for st in stores:
        st.wait()


def local(tokens, cotangent, gate_weight, up_weight, down_weight):
    vmem = pl.BlockSpec(memory_space=pltpu.VMEM)
    hbm = pl.BlockSpec(memory_space=pl.ANY)
    small = jax.ShapeDtypeStruct((LOCAL, W), BF16)
    big = jax.ShapeDtypeStruct((W, W), BF16)
    results = pl.pallas_call(
        functools.partial(kernel, PLAN),
        name="swiglu",
        out_shape=(small, small, big, big, big),
        in_specs=[vmem, vmem, hbm, hbm, hbm],
        out_specs=(vmem, vmem, hbm, hbm, hbm),
        scratch_shapes=[
            pltpu.VMEM((W, W), BF16),
            pltpu.VMEM((W, W), BF16),
            pltpu.VMEM((W, W), BF16),
            pltpu.VMEM((2, 6, 4, 4, 16, HALF), BF16),
            pltpu.VMEM((2, W, W), BF16),
            pltpu.VMEM((3, W, HALF), F32),
            pltpu.VMEM((3, W, HALF), F32),
            pltpu.VMEM((3, W, HALF), F32),
            pltpu.VMEM((3, 3, W // 4, HALF), BF16),
            pltpu.VMEM((3, 3, W // 4, HALF), BF16),
            pltpu.VMEM((3, W, W), BF16),
            pltpu.VMEM((2, 6, 4, 4, 16, HALF), F32),
            pltpu.VMEM((2, 6, 4, 4, 16, HALF), BF16),
            pltpu.VMEM((2, 3, 6, 4, 16, HALF), BF16),
            pltpu.VMEM((max(SIZES), 4, 16, HALF), F32),
            pltpu.VMEM((2, 6, 4, 16, HALF), BF16),
            pltpu.VMEM((2, 6, 16, HALF), F32),
            pltpu.VMEM((2, 3, 6, 16, HALF), BF16),
            pltpu.VMEM((2, 6, 16, HALF), F32),
            pltpu.VMEM((2, 3, 16, HALF), F32),
            pltpu.VMEM((3, W, W), BF16),
            pltpu.SemaphoreType.DMA((SENDS,)),
            pltpu.SemaphoreType.DMA((RECVS,)),
            pltpu.SemaphoreType.DMA((3,)),
            pltpu.SemaphoreType.DMA((3,)),
        ],
        compiler_params=pltpu.CompilerParams(
            collective_id=0, has_side_effects=True, vmem_limit_bytes=56 << 20),
        cost_estimate=pl.CostEstimate(
            flops=18 * W ** 3, bytes_accessed=12 * W * W, transcendentals=W * W // 8),
    )(tokens, cotangent, gate_weight, up_weight, down_weight)
    return pl.pallas_call(
        move,
        name="move",
        out_shape=(small, small, big, big, big),
        in_specs=[hbm] * 5,
        out_specs=(hbm,) * 5,
        scratch_shapes=[pltpu.VMEM((LOCAL, W), BF16)] * 2 + [pltpu.VMEM((W, W), BF16)] * 3
        + [pltpu.SemaphoreType.DMA((14,))] * 2,
        compiler_params=pltpu.CompilerParams(vmem_limit_bytes=60 << 20),
    )(*results)


def solution(mesh):
    by_token = P(("depth", "col"), "row")
    by_model = P("row", ("depth", "col"))
    return jax.shard_map(
        local,
        mesh=mesh,
        in_specs=(by_token, by_token, by_model, by_model, by_token),
        out_specs=(by_token, by_token, by_model, by_model, by_token),
        check_vma=False,
    )
```

time: 228 us -> 108 us (0.47)
  the two profiles are of different devices: /device:TPU:1 before, /device:TPU:32 now
where the time goes in v3:
time: 108 us
  Pallas kernels  108 us (100%)
    pallas_call x1, Pallas kernels, local(): pl.pallas_call(functools.partial(kernel, PLAN), name='swiglu', out_shape=...  104 us
    pallas_call x1, Pallas kernels, local(): pl.pallas_call(move, name='move', out_shape=(small, small, big, big, big)...  3.13 us

profile of v3, /device:TPU:32, one launch (start us, length us, event | category | flops | bytes accessed | tf_op | source)
XLA Modules:
  0.0 108.2 jit_solution(13415178699821514251)
XLA Ops:
  0.6 104.4 %swiglu.1 = (bf16[24,768]{1,0:T(8,128)(2,1)}, bf16[24,768]{1,0:T(8,128)(2,1)}, bf16[768,768]{1,0:T(8,128)(2,1)}, bf16[768,768]{1,0:T(8,128)(2,1)}, bf16[768,768]{1,0:T(8,128)(2,1)}) custom-call(bf16[24,768]{1,0:T(8,128)(2,1)} %x_in.1, bf16[24,768]{1,0:T(8,128)(2,1)} %c_in.1, bf16[768,768]{1,0:T(8,128)(2,1)} %wg_hbm.1, bf16[768,768]{1,0:T(8,128)(2,1)} %wu_hbm.1, ...), custom_call_target="tpu_custom_call" | custom-call | flops 8153726976 | bytes 7077888 | tf_op jit(solution)/shard_map/swiglu/pallas_call | solution.py:359
  105.1 3.1 %move.1 = (bf16[24,768]{1,0:T(8,128)(2,1)}, bf16[24,768]{1,0:T(8,128)(2,1)}, bf16[768,768]{1,0:T(8,128)(2,1)}, bf16[768,768]{1,0:T(8,128)(2,1)}, bf16[768,768]{1,0:T(8,128)(2,1)}) custom-call(bf16[24,768]{1,0:T(8,128)(2,1)} %get-tuple-element.10.refs_0_, bf16[24,768]{1,0:T(8,128)(2,1)} %get-tuple-element.11.refs_1_, ...), custom_call_target="tpu_custom_call" | custom-call | tf_op jit(solution)/shard_map/move/pallas_call | solution.py:397

commit v4 on v3

--- a/solution.py
+++ b/solution.py
@@ -14,9 +14,9 @@
 LOCAL = 24
 UNIT = 128
 
-SIZES = (1, 1, 2, 1, 1)
-OWN = (0, 4, 5)
-OTHER = (1, 2, 3)
+SIZES = (1, 1, 1, 1, 1, 1)
+OWN = (0, 1, 5)
+OTHER = (2, 3, 4)
 
 X1, C1, X2, C2, CORE, ZA, ZB, ZC, GN, GP, GF, GC, O1, G1, O2, G2 = range(16)
 KINDS = 16
@@ -24,23 +24,29 @@
 SENDS = KINDS + 2
 RECVS = KINDS * len(SIZES) + 4
 
+DIRECT = (5,)
+
 PLAN = (
-    ("ag1", 3), ("ag1", 0), ("ready", 0), ("ag1", 4), ("zl_send", 0), ("zl_send", 2),
-    ("ag2c", 3), ("ag2x", 3), ("zl_send", 1), ("ag2x", 0), ("ag2c", 0), ("ag1", 1),
-    ("mmc", 3), ("mmx", 3), ("mmx", 0), ("rs1", 3), ("ag1", 2), ("ag2x", 1),
-    ("ag2c", 1), ("mmc", 0), ("rs1", 0), ("rs2", 3), ("ag2c", 4), ("mmc", 1),
-    ("mmx", 1), ("ag2c", 2), ("ag2x", 2), ("rs2", 0), ("rs1", 1), ("el", 3),
-    ("rs2", 1), ("el", 0), ("mmc", 2), ("ag2x", 4), ("mmx", 2), ("fw", 3),
-    ("rs1", 2), ("fp", 3), ("fw2", 3), ("el", 1), ("outa", 3), ("fp", 0),
-    ("mmc", 4), ("outb", 3), ("fw", 0), ("mmx", 4), ("rs2", 2), ("fp", 1),
-    ("fw", 1), ("rs1", 4), ("fw2", 0), ("el", 2), ("fw2", 1), ("outa", 1),
-    ("outa", 0), ("o2b", 3), ("rs2", 4), ("outb", 0), ("outb", 1), ("fw", 2),
-    ("o2a", 1), ("el", 4), ("o3b", 3), ("fp", 2), ("fw2", 2), ("fw", 4),
-    ("outa", 2), ("outb", 2), ("o2a", 0), ("o2b", 1), ("fp", 4), ("fw2", 4),
-    ("outa", 4), ("o2a", 2), ("o3b", 1), ("o2a", 3), ("o2b", 2), ("outb", 4),
-    ("grad", 2), ("o3a", 2), ("o2b", 0), ("o2a", 4), ("o3a", 1), ("o3b", 2),
-    ("fin_send", 0), ("grad", 1), ("o2b", 4), ("grad", 0), ("o3b", 0), ("o3a", 3),
-    ("o3a", 4), ("o3a", 0), ("o3b", 4), ("sent", 0), ("end", 0),
+    ("ag1", 1), ("ready", 0), ("ag1", 0), ("ag2x", 1), ("zl_send", 1), ("ag2c", 1),
+    ("ag1", 3), ("zl_send", 2), ("ag2x", 0), ("ag2c", 0), ("zl_send", 0), ("mmx", 1),
+    ("mmc", 1), ("ag2c", 3), ("ag1", 2), ("rs1", 1), ("ag2x", 3), ("mmc", 0),
+    ("mmx", 0), ("ag2c", 2), ("rs1", 0), ("ag1", 4), ("ag1", 5), ("mmc", 3),
+    ("ag2x", 2), ("mmx", 3), ("rs2", 1), ("rs1", 3), ("mmx", 2), ("rs2", 0),
+    ("mmc", 2), ("rs1", 2), ("rs2", 3), ("el", 1), ("el", 0), ("ag2x", 5),
+    ("ag2c", 5), ("ag2x", 4), ("ag2c", 4), ("rs2", 2), ("fw", 1), ("mmc", 5),
+    ("el", 3), ("fp", 1), ("mmc", 4), ("mmx", 4), ("rs1", 4), ("fw2", 1),
+    ("fp", 0), ("fw", 0), ("mmx", 5), ("fp", 3), ("outa", 1), ("el", 2),
+    ("outb", 1), ("o2a", 1), ("rs2", 4), ("fw", 3), ("fw", 2), ("fw2", 0),
+    ("rs1", 5), ("outa", 0), ("el", 4), ("fp", 2), ("outb", 0), ("o2a", 0),
+    ("fw2", 3), ("outa", 3), ("fw2", 2), ("rs2", 5), ("outb", 3), ("outa", 2),
+    ("fw", 4), ("grad0", 0), ("el", 5), ("fp", 4), ("o2b", 3), ("outb", 2),
+    ("grad1", 0), ("fw2", 4), ("o2b", 0), ("o2b", 1), ("o3a", 0), ("outa", 4),
+    ("outb", 4), ("grad2", 0), ("o3b", 0), ("o2b", 2), ("fp", 5), ("o2a", 2),
+    ("o3a", 1), ("fw", 5), ("o2a", 3), ("o3b", 3), ("fw2", 5), ("o2b", 4),
+    ("o3b", 2), ("o2a", 4), ("outa", 5), ("outb", 5), ("o3a", 2), ("grad0", 1),
+    ("o3a", 4), ("o3b", 1), ("o3a", 3), ("o3b", 4), ("fin_send", 0), ("o2a", 5),
+    ("o2b", 5), ("grad2", 1), ("grad1", 1), ("o3a", 5), ("o3b", 5), ("sent", 0),
+    ("end", 0),
 )
 
 
@@ -66,11 +72,11 @@
     return v.reshape(v.shape[0] * 8, W)
 
 
-def kernel(plan, x_in, c_in, wg_hbm, wu_hbm, wd_hbm,
-           out_ref, gt_ref, gg_hbm, gu_hbm, gd_hbm,
-           wg, wu, wd, xc, xg, csnd, crcv, part, zsnd, zrcv, hid,
+def kernel(plan, x_hbm, c_hbm, wg_hbm, wu_hbm, wd_hbm,
+           out_ref, gt_ref, gg, gu, gd,
+           x_in, c_in, acc, wg, wu, wd, xc, xg, csnd, crcv, part, zsnd, zrcv, hid,
            pf, psnd, p1rcv, sf, s1snd, s1own, p2rcv, fin, frcv,
-           grads, ssem, rsem, lsem, gsem):
+           ssem, rsem, lsem):
     depth, row, xx = lax.axis_index("depth"), lax.axis_index("row"), lax.axis_index("col")
     zl, y, zh, a = depth // 4, depth % 4, row // 2, row % 2
     nxt, prv, opp = (zh + 1 + 2 * a) % 4, (zh + 3 + 2 * a) % 4, (zh + 2) % 4
@@ -78,7 +84,7 @@
     def dev(zl_=zl, y_=y, zh_=zh, a_=a, x_=xx):
         return (zl_ * 4 + y_, zh_ * 2 + a_, x_)
 
-    others = ([dev(zl_=1 - zl), dev(a_=1 - a), dev(zh_=nxt), dev(zh_=prv)]
+    others = ([dev(zl_=1 - zl), dev(a_=1 - a), dev(zh_=nxt), dev(zh_=prv), dev(zh_=opp)]
               + [dev(x_=(xx + j) % 4) for j in (1, 2, 3)]
               + [dev(y_=(y + j) % 4) for j in (1, 2, 3)])
     mine = pl.ds(pl.multiple_of(a * HALF, 128), HALF)
@@ -112,14 +118,16 @@
 
     last = KINDS * len(SIZES)
 
-    loads = [pltpu.make_async_copy(s, d, lsem.at[j])
-             for j, (s, d) in enumerate(((wg_hbm, wg), (wu_hbm, wu), (wd_hbm, wd)))]
-    for ld in loads:
-        ld.start()
     barrier = pltpu.get_barrier_semaphore()
     for o in others:
         pl.semaphore_signal(barrier, inc=1, device_id=o, device_id_type=pl.DeviceIdType.MESH)
+    loads = [pltpu.make_async_copy(s, d, lsem.at[j])
+             for j, (s, d) in enumerate(((x_hbm, x_in), (c_hbm, c_in), (wg_hbm, wg),
+                                         (wu_hbm, wu), (wd_hbm, wd)))]
+    for ld in loads:
+        ld.start()
     for k, ref in enumerate((x_in, c_in)):
+        loads[k].wait()
         v = fold(ref[...].astype(F32)).astype(BF16)
         for u in range(3):
             xc[k, OWN[u], y, xx] = v[u]
@@ -155,7 +163,7 @@
             send(i, C2, blk, blk, dev(x_=(xx + j) % 4))
 
     def ready(_):
-        for ld in loads:
+        for ld in loads[2:]:
             ld.wait()
 
     def gathered(i, k):
@@ -211,12 +219,15 @@
         blk = hid.at[:, ps, mine]
         send(i, GN, blk, blk, dev(zh_=nxt))
         send(i, GP, blk, blk, dev(zh_=prv))
+        if i in DIRECT:
+            send(i, GF, blk, blk, dev(zh_=opp))
         send(i, GC, blk, blk, dev(a_=1 - a))
 
     def fw(i):
         blk = hid.at[:, piece(i, prv), mine]
         got(i, GN, blk)
-        send(i, GF, blk, blk, dev(zh_=nxt))
+        if i not in DIRECT:
+            send(i, GF, blk, blk, dev(zh_=nxt))
         send(i, GC, blk, blk, dev(a_=1 - a))
 
     def fp(i):
@@ -300,21 +311,31 @@
             wait(ssem.at[k], ref)
 
     scale = W ** -0.5
-    stores = []
-
-    def grad(which):
-        lhs, k, hbm = ((xg.at[0], 1, gg_hbm), (xg.at[0], 2, gu_hbm), (hid.at[0], 0, gd_hbm))[which]
+
+    def grads(i, which):
+        rs = slice(512 * i, 512 + 256 * i)
+        lhs, rhs, res = ((xg.at[0, rs], hid[1, rs], gg), (xg.at[0, rs], hid[2, rs], gu),
+                         (hid.at[0, rs], xg[1, rs], gd))[which]
 
         def tile(n, _):
             ds = pl.ds(pl.multiple_of(n * 256, 256), 256)
-            rhs = hid[k] if which < 2 else xg[1]
-            grads[which, ds, :] = (tn(lhs[:, ds], rhs) * scale).astype(BF16)
+            t = tn(lhs[:, ds], rhs)
+            if i == 0:
+                acc[which, ds, :] = t
+            else:
+                res[ds, :] = ((t + acc[which, ds, :]) * scale).astype(BF16)
             return _
 
         lax.fori_loop(0, 3, tile, 0)
-        st = pltpu.make_async_copy(grads.at[which], hbm, gsem.at[which])
-        st.start()
-        stores.append(st)
+
+    def grad0(i):
+        grads(i, 0)
+
+    def grad1(i):
+        grads(i, 1)
+
+    def grad2(i):
+        grads(i, 2)
 
     def end(_):
         wait(rsem.at[last + FIN], frcv)
@@ -324,28 +345,15 @@
 
     steps = {f.__name__: f for f in (
         zl_send, ag1, ag2x, ag2c, ready, mmx, mmc, rs1, rs2, el, fw, fp, fw2, outa, outb,
-        o2a, o2b, o3a, o3b, fin_send, sent, grad, end)}
+        o2a, o2b, o3a, o3b, fin_send, sent, grad0, grad1, grad2, end)}
     for name, i in plan:
         steps[name](i)
+
+
+def move(*refs):
+    stores = [pltpu.make_async_copy(s, d, refs[10].at[n])
+              for n, (s, d) in enumerate(zip(refs[:5], refs[5:10]))]
     for st in stores:
-        st.wait()
-
-
-def move(*refs):
-    srcs, dsts, bufs, isem, osem = refs[:5], refs[5:10], refs[10:15], refs[15], refs[16]
-    parts = []
-    for j in (2, 3, 4):
-        for q in range(4):
-            ds = pl.ds(q * W // 4, W // 4)
-            parts.append((srcs[j].at[ds], bufs[j].at[ds], dsts[j].at[ds]))
-    for j in (0, 1):
-        parts.append((srcs[j], bufs[j], dsts[j]))
-    loads = [pltpu.make_async_copy(s, b, isem.at[n]) for n, (s, b, _) in enumerate(parts)]
-    stores = [pltpu.make_async_copy(b, d, osem.at[n]) for n, (_, b, d) in enumerate(parts)]
-    for ld in loads:
-        ld.start()
-    for ld, st in zip(loads, stores):
-        ld.wait()
         st.start()
     for st in stores:
         st.wait()
@@ -359,10 +367,13 @@
     results = pl.pallas_call(
         functools.partial(kernel, PLAN),
         name="swiglu",
-        out_shape=(small, small, big, big, big),
-        in_specs=[vmem, vmem, hbm, hbm, hbm],
-        out_specs=(vmem, vmem, hbm, hbm, hbm),
+        out_shape=[pltpu.VMEM(t.shape, t.dtype) for t in (small, small, big, big, big)],
+        in_specs=[hbm] * 5,
+        out_specs=[vmem] * 5,
         scratch_shapes=[
+            pltpu.VMEM((LOCAL, W), BF16),
+            pltpu.VMEM((LOCAL, W), BF16),
+            pltpu.VMEM((3, W, W), F32),
             pltpu.VMEM((W, W), BF16),
             pltpu.VMEM((W, W), BF16),
             pltpu.VMEM((W, W), BF16),
@@ -383,11 +394,9 @@
             pltpu.VMEM((2, 3, 6, 16, HALF), BF16),
             pltpu.VMEM((2, 6, 16, HALF), F32),
             pltpu.VMEM((2, 3, 16, HALF), F32),
-            pltpu.VMEM((3, W, W), BF16),
             pltpu.SemaphoreType.DMA((SENDS,)),
             pltpu.SemaphoreType.DMA((RECVS,)),
-            pltpu.SemaphoreType.DMA((3,)),
-            pltpu.SemaphoreType.DMA((3,)),
+            pltpu.SemaphoreType.DMA((5,)),
         ],
         compiler_params=pltpu.CompilerParams(
             collective_id=0, has_side_effects=True, vmem_limit_bytes=56 << 20),
@@ -398,11 +407,9 @@
         move,
         name="move",
         out_shape=(small, small, big, big, big),
-        in_specs=[hbm] * 5,
+        in_specs=[vmem] * 5,
         out_specs=(hbm,) * 5,
-        scratch_shapes=[pltpu.VMEM((LOCAL, W), BF16)] * 2 + [pltpu.VMEM((W, W), BF16)] * 3
-        + [pltpu.SemaphoreType.DMA((14,))] * 2,
-        compiler_params=pltpu.CompilerParams(vmem_limit_bytes=60 << 20),
+        scratch_shapes=[pltpu.SemaphoreType.DMA((5,))],
     )(*results)
 
 

time: 108 us -> 111 us (1.028)
  local copies, waits for them, and re-layouts: 0 us -> 4.28 us
  Pallas kernels: 108 us -> 106 us
    unnamed x0 -> x10, local copies, waits for them, and re-layouts: none -> 4.28 us
    pallas_call x1, Pallas kernels: 104 us -> 102 us  [local(): pl.pallas_call(functools.partial(kernel, PLAN), name='swiglu', out_shape=...]
where the time goes in v4:
time: 111 us
  Pallas kernels  106 us (95%)
  local copies, waits for them, and re-layouts  4.28 us (4%)
    pallas_call x1, Pallas kernels, local(): pl.pallas_call(functools.partial(kernel, PLAN), name='swiglu', out_shape=...  102 us
    unnamed x10, local copies, waits for them, and re-layouts  4.28 us
    pallas_call x1, Pallas kernels, local(): pl.pallas_call(move, name='move', out_shape=(small, small, big, big, big)...  3.87 us

profile of v4, /device:TPU:32, one launch (start us, length us, event | category | flops | bytes accessed | tf_op | source)
XLA Modules:
  0.0 110.9 jit_solution(10934129411150705320)
XLA Ops:
  0.6 101.9 %swiglu.1 = (bf16[24,768]{1,0:T(8,128)(2,1)S(1)}, bf16[24,768]{1,0:T(8,128)(2,1)S(1)}, bf16[768,768]{1,0:T(8,128)(2,1)S(1)}, bf16[768,768]{1,0:T(8,128)(2,1)S(1)}, bf16[768,768]{1,0:T(8,128)(2,1)S(1)}) custom-call(bf16[24,768]{1,0:T(8,128)(2,1)} %x_hbm.1, bf16[24,768]{1,0:T(8,128)(2,1)} %c_hbm.1, bf16[768,768]{1,0:T(8,128)(2,1)} %wg_hbm.1, ...), custom_call_target="tpu_custom_call" | custom-call | flops 8153726976 | bytes 7077888 | tf_op jit(solution)/shard_map/swiglu/pallas_call | solution.py:367
  102.6 0.0 copy-start
  102.6 1.0 copy-done
  103.6 0.0 copy-start.1
  103.6 1.0 copy-done.1
  104.6 0.0 copy-start.2
  104.6 1.0 copy-done.2
  105.7 0.0 copy-start.3
  105.7 0.6 copy-done.3
  106.3 0.0 copy-start.4
  106.3 0.6 copy-done.4
  106.9 3.9 %move.1 = (bf16[24,768]{1,0:T(8,128)(2,1)}, bf16[24,768]{1,0:T(8,128)(2,1)}, bf16[768,768]{1,0:T(8,128)(2,1)}, bf16[768,768]{1,0:T(8,128)(2,1)}, bf16[768,768]{1,0:T(8,128)(2,1)}) custom-call(bf16[24,768]{1,0:T(8,128)(2,1)} %copy-done.3, bf16[24,768]{1,0:T(8,128)(2,1)} %copy-done.4, bf16[768,768]{1,0:T(8,128)(2,1)} %copy-done, bf16[768,768]{1,0:T(8,128)(2,1)} %copy-done.1, ...), custom_call_target="tpu_custom_call" | custom-call | tf_op jit(solution)/shard_map/move/pallas_call | solution.py:406
Async XLA Ops:
  102.6 1.0 copy-start
  103.6 1.0 copy-start.1
  104.6 1.0 copy-start.2
  105.7 0.6 copy-start.3
  106.3 0.6 copy-start.4

commit v5 on v4

--- a/solution.py
+++ b/solution.py
@@ -15,8 +15,8 @@
 UNIT = 128
 
 SIZES = (1, 1, 1, 1, 1, 1)
-OWN = (0, 1, 5)
-OTHER = (2, 3, 4)
+OWN = (0, 4, 5)
+OTHER = (1, 2, 3)
 
 X1, C1, X2, C2, CORE, ZA, ZB, ZC, GN, GP, GF, GC, O1, G1, O2, G2 = range(16)
 KINDS = 16
@@ -24,28 +24,28 @@
 SENDS = KINDS + 2
 RECVS = KINDS * len(SIZES) + 4
 
-DIRECT = (5,)
+DIRECT = ()
 
 PLAN = (
-    ("ag1", 1), ("ready", 0), ("ag1", 0), ("ag2x", 1), ("zl_send", 1), ("ag2c", 1),
-    ("ag1", 3), ("zl_send", 2), ("ag2x", 0), ("ag2c", 0), ("zl_send", 0), ("mmx", 1),
-    ("mmc", 1), ("ag2c", 3), ("ag1", 2), ("rs1", 1), ("ag2x", 3), ("mmc", 0),
-    ("mmx", 0), ("ag2c", 2), ("rs1", 0), ("ag1", 4), ("ag1", 5), ("mmc", 3),
-    ("ag2x", 2), ("mmx", 3), ("rs2", 1), ("rs1", 3), ("mmx", 2), ("rs2", 0),
-    ("mmc", 2), ("rs1", 2), ("rs2", 3), ("el", 1), ("el", 0), ("ag2x", 5),
-    ("ag2c", 5), ("ag2x", 4), ("ag2c", 4), ("rs2", 2), ("fw", 1), ("mmc", 5),
-    ("el", 3), ("fp", 1), ("mmc", 4), ("mmx", 4), ("rs1", 4), ("fw2", 1),
-    ("fp", 0), ("fw", 0), ("mmx", 5), ("fp", 3), ("outa", 1), ("el", 2),
-    ("outb", 1), ("o2a", 1), ("rs2", 4), ("fw", 3), ("fw", 2), ("fw2", 0),
-    ("rs1", 5), ("outa", 0), ("el", 4), ("fp", 2), ("outb", 0), ("o2a", 0),
-    ("fw2", 3), ("outa", 3), ("fw2", 2), ("rs2", 5), ("outb", 3), ("outa", 2),
-    ("fw", 4), ("grad0", 0), ("el", 5), ("fp", 4), ("o2b", 3), ("outb", 2),
-    ("grad1", 0), ("fw2", 4), ("o2b", 0), ("o2b", 1), ("o3a", 0), ("outa", 4),
-    ("outb", 4), ("grad2", 0), ("o3b", 0), ("o2b", 2), ("fp", 5), ("o2a", 2),
-    ("o3a", 1), ("fw", 5), ("o2a", 3), ("o3b", 3), ("fw2", 5), ("o2b", 4),
-    ("o3b", 2), ("o2a", 4), ("outa", 5), ("outb", 5), ("o3a", 2), ("grad0", 1),
-    ("o3a", 4), ("o3b", 1), ("o3a", 3), ("o3b", 4), ("fin_send", 0), ("o2a", 5),
-    ("o2b", 5), ("grad2", 1), ("grad1", 1), ("o3a", 5), ("o3b", 5), ("sent", 0),
+    ("zl_send", 0), ("ag1", 5), ("zl_send", 1), ("zl_send", 2), ("ag1", 4), ("ag1", 0),
+    ("ready", 0), ("ag1", 1), ("ag2c", 5), ("ag2x", 5), ("ag2x", 1), ("ag2c", 1),
+    ("mmc", 5), ("mmx", 5), ("ag1", 2), ("ag2x", 4), ("ag2c", 4), ("mmx", 1),
+    ("rs1", 5), ("mmc", 1), ("ag1", 3), ("ag2c", 0), ("ag2x", 2), ("rs1", 1),
+    ("mmx", 4), ("ag2x", 3), ("mmc", 4), ("rs2", 5), ("ag2c", 2), ("mmc", 0),
+    ("rs1", 4), ("rs2", 1), ("mmx", 3), ("mmx", 2), ("mmc", 2), ("el", 5),
+    ("ag2x", 0), ("ag2c", 3), ("rs1", 2), ("el", 1), ("mmc", 3), ("rs1", 3),
+    ("fw", 5), ("rs2", 2), ("fw", 1), ("mmx", 0), ("rs2", 3), ("rs1", 0),
+    ("fw2", 5), ("el", 2), ("fp", 5), ("fw2", 1), ("fp", 1), ("outa", 1),
+    ("el", 3), ("outb", 1), ("outa", 5), ("rs2", 4), ("fw", 2), ("fp", 2),
+    ("outb", 5), ("rs2", 0), ("fw", 3), ("o2b", 1), ("fp", 3), ("o2a", 1),
+    ("o2a", 5), ("el", 4), ("o3a", 1), ("fw2", 2), ("el", 0), ("outa", 2),
+    ("fw2", 3), ("o2b", 5), ("outb", 2), ("outa", 3), ("fw", 4), ("fp", 4),
+    ("outb", 3), ("o3b", 1), ("fw", 0), ("o2a", 2), ("fw2", 4), ("o2b", 2),
+    ("fp", 0), ("o2a", 3), ("o3a", 5), ("o2b", 3), ("fw2", 0), ("outa", 4),
+    ("outb", 4), ("outa", 0), ("grad2", 0), ("outb", 0), ("o3a", 2), ("o3a", 3),
+    ("o3b", 2), ("o3b", 3), ("fin_send", 0), ("grad1", 0), ("grad2", 1), ("o2a", 4),
+    ("o2b", 4), ("grad1", 1), ("o2a", 0), ("o3b", 5), ("o2b", 0), ("grad0", 0),
+    ("o3a", 4), ("grad0", 1), ("o3a", 0), ("o3b", 0), ("o3b", 4), ("sent", 0),
     ("end", 0),
 )
 
@@ -73,10 +73,10 @@
 
 
 def kernel(plan, x_hbm, c_hbm, wg_hbm, wu_hbm, wd_hbm,
-           out_ref, gt_ref, gg, gu, gd,
-           x_in, c_in, acc, wg, wu, wd, xc, xg, csnd, crcv, part, zsnd, zrcv, hid,
+           out_ref, gt_ref, gg_hbm, gu_hbm, gd_hbm,
+           x_in, c_in, acc, grad, wg, wu, wd, xc, xg, csnd, crcv, part, zsnd, zrcv, hid,
            pf, psnd, p1rcv, sf, s1snd, s1own, p2rcv, fin, frcv,
-           ssem, rsem, lsem):
+           ssem, rsem, lsem, gsem):
     depth, row, xx = lax.axis_index("depth"), lax.axis_index("row"), lax.axis_index("col")
     zl, y, zh, a = depth // 4, depth % 4, row // 2, row % 2
     nxt, prv, opp = (zh + 1 + 2 * a) % 4, (zh + 3 + 2 * a) % 4, (zh + 2) % 4
@@ -311,11 +311,12 @@
             wait(ssem.at[k], ref)
 
     scale = W ** -0.5
+    stores = []
 
     def grads(i, which):
         rs = slice(512 * i, 512 + 256 * i)
-        lhs, rhs, res = ((xg.at[0, rs], hid[1, rs], gg), (xg.at[0, rs], hid[2, rs], gu),
-                         (hid.at[0, rs], xg[1, rs], gd))[which]
+        lhs, rhs, res = ((xg.at[0, rs], hid[1, rs], gg_hbm), (xg.at[0, rs], hid[2, rs], gu_hbm),
+                         (hid.at[0, rs], xg[1, rs], gd_hbm))[which]
 
         def tile(n, _):
             ds = pl.ds(pl.multiple_of(n * 256, 256), 256)
@@ -323,10 +324,14 @@
             if i == 0:
                 acc[which, ds, :] = t
             else:
-                res[ds, :] = ((t + acc[which, ds, :]) * scale).astype(BF16)
+                grad[which, ds, :] = ((t + acc[which, ds, :]) * scale).astype(BF16)
             return _
 
         lax.fori_loop(0, 3, tile, 0)
+        if i == 1:
+            st = pltpu.make_async_copy(grad.at[which], res, gsem.at[which])
+            st.start()
+            stores.append(st)
 
     def grad0(i):
         grads(i, 0)
@@ -348,12 +353,25 @@
         o2a, o2b, o3a, o3b, fin_send, sent, grad0, grad1, grad2, end)}
     for name, i in plan:
         steps[name](i)
+    for st in stores:
+        st.wait()
 
 
 def move(*refs):
-    stores = [pltpu.make_async_copy(s, d, refs[10].at[n])
-              for n, (s, d) in enumerate(zip(refs[:5], refs[5:10]))]
-    for st in stores:
+    srcs, dsts, bufs, isem, osem = refs[:5], refs[5:10], refs[10:15], refs[15], refs[16]
+    parts = []
+    for j in (2, 3, 4):
+        for q in range(2):
+            ds = pl.ds(q * HALF, HALF)
+            parts.append((srcs[j].at[ds], bufs[j].at[ds], dsts[j].at[ds]))
+    for j in (0, 1):
+        parts.append((srcs[j], bufs[j], dsts[j]))
+    loads = [pltpu.make_async_copy(s, b, isem.at[n]) for n, (s, b, _) in enumerate(parts)]
+    stores = [pltpu.make_async_copy(b, d, osem.at[n]) for n, (_, b, d) in enumerate(parts)]
+    for ld in loads:
+        ld.start()
+    for ld, st in zip(loads, stores):
+        ld.wait()
         st.start()
     for st in stores:
         st.wait()
@@ -367,13 +385,14 @@
     results = pl.pallas_call(
         functools.partial(kernel, PLAN),
         name="swiglu",
-        out_shape=[pltpu.VMEM(t.shape, t.dtype) for t in (small, small, big, big, big)],
+        out_shape=(small, small, big, big, big),
         in_specs=[hbm] * 5,
-        out_specs=[vmem] * 5,
+        out_specs=(vmem, vmem, hbm, hbm, hbm),
         scratch_shapes=[
             pltpu.VMEM((LOCAL, W), BF16),
             pltpu.VMEM((LOCAL, W), BF16),
             pltpu.VMEM((3, W, W), F32),
+            pltpu.VMEM((3, W, W), BF16),
             pltpu.VMEM((W, W), BF16),
             pltpu.VMEM((W, W), BF16),
             pltpu.VMEM((W, W), BF16),
@@ -397,6 +416,7 @@
             pltpu.SemaphoreType.DMA((SENDS,)),
             pltpu.SemaphoreType.DMA((RECVS,)),
             pltpu.SemaphoreType.DMA((5,)),
+            pltpu.SemaphoreType.DMA((3,)),
         ],
         compiler_params=pltpu.CompilerParams(
             collective_id=0, has_side_effects=True, vmem_limit_bytes=56 << 20),
@@ -407,9 +427,11 @@
         move,
         name="move",
         out_shape=(small, small, big, big, big),
-        in_specs=[vmem] * 5,
+        in_specs=[hbm] * 5,
         out_specs=(hbm,) * 5,
-        scratch_shapes=[pltpu.SemaphoreType.DMA((5,))],
+        scratch_shapes=[pltpu.VMEM((LOCAL, W), BF16)] * 2 + [pltpu.VMEM((W, W), BF16)] * 3
+        + [pltpu.SemaphoreType.DMA((8,))] * 2,
+        compiler_params=pltpu.CompilerParams(vmem_limit_bytes=60 << 20),
     )(*results)
 
 

time: 111 us -> 103 us (0.928)
  local copies, waits for them, and re-layouts: 4.28 us -> 0 us
  Pallas kernels: 106 us -> 102 us
    unnamed x10 -> x0, local copies, waits for them, and re-layouts: 4.28 us -> none
    pallas_call x1, Pallas kernels: 102 us -> 98.9 us  [local(): pl.pallas_call(functools.partial(kernel, PLAN), name='swiglu', out_shape=...]
where the time goes in v5:
time: 103 us
  Pallas kernels  102 us (99%)
    pallas_call x1, Pallas kernels, local(): pl.pallas_call(functools.partial(kernel, PLAN), name='swiglu', out_shape=...  98.9 us
    pallas_call x1, Pallas kernels, local(): pl.pallas_call(move, name='move', out_shape=(small, small, big, big, big)...  3 us

profile of v5, /device:TPU:32, one launch (start us, length us, event | category | flops | bytes accessed | tf_op | source)
XLA Modules:
  0.0 102.7 jit_solution(5658491156091280976)
XLA Ops:
  0.6 98.9 %swiglu.1 = (bf16[24,768]{1,0:T(8,128)(2,1)}, bf16[24,768]{1,0:T(8,128)(2,1)}, bf16[768,768]{1,0:T(8,128)(2,1)}, bf16[768,768]{1,0:T(8,128)(2,1)}, bf16[768,768]{1,0:T(8,128)(2,1)}) custom-call(bf16[24,768]{1,0:T(8,128)(2,1)} %x_hbm.1, bf16[24,768]{1,0:T(8,128)(2,1)} %c_hbm.1, bf16[768,768]{1,0:T(8,128)(2,1)} %wg_hbm.1, bf16[768,768]{1,0:T(8,128)(2,1)} %wu_hbm.1, ...), custom_call_target="tpu_custom_call" | custom-call | flops 8153726976 | bytes 7077888 | tf_op jit(solution)/shard_map/swiglu/pallas_call | solution.py:385
  99.5 3.0 %move.1 = (bf16[24,768]{1,0:T(8,128)(2,1)}, bf16[24,768]{1,0:T(8,128)(2,1)}, bf16[768,768]{1,0:T(8,128)(2,1)}, bf16[768,768]{1,0:T(8,128)(2,1)}, bf16[768,768]{1,0:T(8,128)(2,1)}) custom-call(bf16[24,768]{1,0:T(8,128)(2,1)} %get-tuple-element.10.refs_0_, bf16[24,768]{1,0:T(8,128)(2,1)} %get-tuple-element.11.refs_1_, ...), custom_call_target="tpu_custom_call" | custom-call | tf_op jit(solution)/shard_map/move/pallas_call | solution.py:426

commit v6 on v5

--- a/solution.py
+++ b/solution.py
@@ -14,39 +14,42 @@
 LOCAL = 24
 UNIT = 128
 
-SIZES = (1, 1, 1, 1, 1, 1)
 OWN = (0, 4, 5)
 OTHER = (1, 2, 3)
+WHOLE, NEAR, FAR = range(3)
+CHUNKS = ((0, NEAR), (0, FAR), (1, WHOLE), (2, WHOLE), (3, WHOLE), (4, WHOLE), (5, WHOLE))
 
 X1, C1, X2, C2, CORE, ZA, ZB, ZC, GN, GP, GF, GC, O1, G1, O2, G2 = range(16)
 KINDS = 16
 ZL, FIN = 0, 3
 SENDS = KINDS + 2
-RECVS = KINDS * len(SIZES) + 4
+RECVS = 14 * len(CHUNKS) + 2 * 6 + 4
 
 DIRECT = ()
 
 PLAN = (
-    ("zl_send", 0), ("ag1", 5), ("zl_send", 1), ("zl_send", 2), ("ag1", 4), ("ag1", 0),
-    ("ready", 0), ("ag1", 1), ("ag2c", 5), ("ag2x", 5), ("ag2x", 1), ("ag2c", 1),
-    ("mmc", 5), ("mmx", 5), ("ag1", 2), ("ag2x", 4), ("ag2c", 4), ("mmx", 1),
-    ("rs1", 5), ("mmc", 1), ("ag1", 3), ("ag2c", 0), ("ag2x", 2), ("rs1", 1),
-    ("mmx", 4), ("ag2x", 3), ("mmc", 4), ("rs2", 5), ("ag2c", 2), ("mmc", 0),
-    ("rs1", 4), ("rs2", 1), ("mmx", 3), ("mmx", 2), ("mmc", 2), ("el", 5),
-    ("ag2x", 0), ("ag2c", 3), ("rs1", 2), ("el", 1), ("mmc", 3), ("rs1", 3),
-    ("fw", 5), ("rs2", 2), ("fw", 1), ("mmx", 0), ("rs2", 3), ("rs1", 0),
-    ("fw2", 5), ("el", 2), ("fp", 5), ("fw2", 1), ("fp", 1), ("outa", 1),
-    ("el", 3), ("outb", 1), ("outa", 5), ("rs2", 4), ("fw", 2), ("fp", 2),
-    ("outb", 5), ("rs2", 0), ("fw", 3), ("o2b", 1), ("fp", 3), ("o2a", 1),
-    ("o2a", 5), ("el", 4), ("o3a", 1), ("fw2", 2), ("el", 0), ("outa", 2),
-    ("fw2", 3), ("o2b", 5), ("outb", 2), ("outa", 3), ("fw", 4), ("fp", 4),
-    ("outb", 3), ("o3b", 1), ("fw", 0), ("o2a", 2), ("fw2", 4), ("o2b", 2),
-    ("fp", 0), ("o2a", 3), ("o3a", 5), ("o2b", 3), ("fw2", 0), ("outa", 4),
-    ("outb", 4), ("outa", 0), ("grad2", 0), ("outb", 0), ("o3a", 2), ("o3a", 3),
-    ("o3b", 2), ("o3b", 3), ("fin_send", 0), ("grad1", 0), ("grad2", 1), ("o2a", 4),
-    ("o2b", 4), ("grad1", 1), ("o2a", 0), ("o3b", 5), ("o2b", 0), ("grad0", 0),
-    ("o3a", 4), ("grad0", 1), ("o3a", 0), ("o3b", 0), ("o3b", 4), ("sent", 0),
-    ("end", 0),
+    ("ag1", 0), ("zl_send", 2), ("ag1", 4), ("ag2x", 0), ("ag2c", 0), ("zl_send", 1),
+    ("ready", 0), ("ag2x", 1), ("zl_send", 0), ("ag2c", 1), ("ag1", 3), ("ag2x", 5),
+    ("ag2c", 5), ("mmx", 0), ("mmc", 0), ("ag2x", 4), ("rs1", 0), ("mmc", 1),
+    ("mmx", 1), ("ag2c", 4), ("mmx", 5), ("rs1", 1), ("mmc", 5), ("ag1", 1),
+    ("ag1", 5), ("rs2", 0), ("rs1", 5), ("mmx", 4), ("ag1", 2), ("mmc", 4),
+    ("ag2x", 2), ("rs2", 1), ("ag2c", 2), ("el", 0), ("rs1", 4), ("el", 1),
+    ("rs2", 5), ("mmx", 2), ("ag2x", 3), ("mmc", 2), ("ag2c", 3), ("fw", 0),
+    ("rs1", 2), ("fw", 1), ("mmx", 3), ("rs2", 4), ("mmc", 3), ("el", 5),
+    ("rs2", 2), ("ag2x", 6), ("ag2c", 6), ("rs1", 3), ("fp", 0), ("fw2", 0),
+    ("outa", 0), ("el", 4), ("outb", 0), ("fw", 5), ("fw2", 1), ("fp", 1),
+    ("el", 2), ("mmx", 6), ("mmc", 6), ("fp", 5), ("outa", 1), ("outb", 1),
+    ("rs2", 3), ("fw", 4), ("fw2", 5), ("rs1", 6), ("outa", 5), ("o2a", 0),
+    ("fw", 2), ("o2a", 1), ("fp", 2), ("outb", 5), ("el", 3), ("fp", 4),
+    ("fw2", 4), ("o2b", 0), ("outa", 4), ("o2a", 5), ("rs2", 6), ("outb", 4),
+    ("fw2", 2), ("fw", 3), ("o2b", 4), ("outa", 2), ("fp", 3), ("el", 6),
+    ("outb", 2), ("fw2", 3), ("o2a", 4), ("o3b", 0), ("outa", 3), ("outb", 3),
+    ("fw", 6), ("o3b", 4), ("grad2", 0), ("o2b", 3), ("o3a", 4), ("o2b", 1),
+    ("fp", 6), ("o2a", 2), ("fw2", 6), ("o3a", 3), ("o3a", 0), ("o2a", 3),
+    ("o2b", 2), ("outa", 6), ("outb", 6), ("grad1", 0), ("o3a", 2), ("grad2", 1),
+    ("o3b", 1), ("o3a", 1), ("o3b", 2), ("o3b", 3), ("fin_send", 0), ("grad0", 0),
+    ("o2a", 6), ("o2b", 5), ("grad0", 1), ("grad1", 1), ("o3a", 5), ("o3b", 5),
+    ("sent", 0), ("end", 0),
 )
 
 
@@ -89,18 +92,41 @@
               + [dev(y_=(y + j) % 4) for j in (1, 2, 3)])
     mine = pl.ds(pl.multiple_of(a * HALF, 128), HALF)
     theirs = pl.ds(pl.multiple_of((1 - a) * HALF, 128), HALF)
-    def units(i):
-        return slice(sum(SIZES[:i]), sum(SIZES[:i + 1]))
+    beside = y + 1 - 2 * (y % 2)
+    here, there = 2 * (y // 2), 2 - 2 * (y // 2)
+    size = [UNIT if part == WHOLE else UNIT // 2 for _, part in CHUNKS]
 
     def rows(i):
-        return slice(UNIT * sum(SIZES[:i]), UNIT * sum(SIZES[:i + 1]))
+        return slice(sum(size[:i]), sum(size[:i + 1]))
 
     def quarter(i):
-        return slice(UNIT // 4 * sum(SIZES[:i]), UNIT // 4 * sum(SIZES[:i + 1]))
+        return slice(sum(size[:i]) // 4, sum(size[:i + 1]) // 4)
 
     def piece(i, q):
-        n = UNIT // 4 * SIZES[i]
-        return pl.ds(pl.multiple_of(UNIT * sum(SIZES[:i]) + n * q, 32), n)
+        n = size[i] // 4
+        return pl.ds(pl.multiple_of(sum(size[:i]) + n * q, 16), n)
+
+    def chips(i):
+        return {WHOLE: pl.ds(0, 4), NEAR: pl.ds(here, 2), FAR: pl.ds(there, 2)}[CHUNKS[i][1]]
+
+    def slots(i):
+        return {WHOLE: slice(0, 4), NEAR: slice(0, 2), FAR: slice(2, 4)}[CHUNKS[i][1]]
+
+    def peers(i):
+        return {WHOLE: [((y + j) % 4, j - 1) for j in (1, 2, 3)], NEAR: [(beside, 0)],
+                FAR: [(there, 1 + y % 2), (there + 1, 1 + y % 2)]}[CHUNKS[i][1]]
+
+    def heard(i):
+        return {WHOLE: slice(0, 3), NEAR: slice(0, 1), FAR: slice(1, 3)}[CHUNKS[i][1]]
+
+    def chunks(e):
+        return [i for i, (u, _) in enumerate(CHUNKS) if u == e]
+
+    across = [((xx + j) % 4, j - 1) for j in (1, 2, 3)]
+    order = {}
+
+    def at(i, k):
+        return order.setdefault((i, k), len(order))
 
     def push(ssem_at, rsem_at, src, dst, to):
         pltpu.make_async_remote_copy(
@@ -108,15 +134,15 @@
             device_id=to, device_id_type=pl.DeviceIdType.MESH).start()
 
     def send(i, k, src, dst, to):
-        push(k, KINDS * i + k, src, dst, to)
+        push(k, at(i, k), src, dst, to)
 
     def wait(sem, ref):
         pltpu.make_async_copy(ref, ref, sem).wait()
 
     def got(i, k, ref):
-        wait(rsem.at[KINDS * i + k], ref)
-
-    last = KINDS * len(SIZES)
+        wait(rsem.at[at(i, k)], ref)
+
+    last = RECVS - 4
 
     barrier = pltpu.get_barrier_semaphore()
     for o in others:
@@ -137,44 +163,45 @@
         push(KINDS, last + ZL + u,
              xc.at[:, OWN[u], y, xx], xc.at[:, OTHER[u], y, xx], dev(zl_=1 - zl))
 
-    def ag1(i):
-        es = units(i)
-        for e in range(es.start, es.stop):
-            if e in OTHER:
-                wait(rsem.at[last + ZL + OTHER.index(e)], xc.at[:, e, y, xx])
-        for j in (1, 2, 3):
-            blk = xc.at[0, es, y, xx]
-            send(i, X1, blk, blk, dev(x_=(xx + j) % 4))
-            blk = xc.at[1, es, y, xx]
-            send(i, C1, blk, blk, dev(y_=(y + j) % 4))
+    def ag1(e):
+        if e in OTHER:
+            wait(rsem.at[last + ZL + OTHER.index(e)], xc.at[:, e, y, xx])
+        blk = xc.at[0, e, y, xx]
+        for to, _ in across:
+            send(chunks(e)[0], X1, blk, blk, dev(x_=to))
+        blk = xc.at[1, e, y, xx]
+        for i in chunks(e):
+            for to, _ in peers(i):
+                send(i, C1, blk, blk, dev(y_=to))
 
     def ag2x(i):
-        es = units(i)
-        got(i, X1, xc.at[0, es, y, :3])
-        for j in (1, 2, 3):
-            blk = xc.at[0, es, y]
-            send(i, X2, blk, blk, dev(y_=(y + j) % 4))
+        e = CHUNKS[i][0]
+        if i == chunks(e)[0]:
+            got(i, X1, xc.at[0, e, y, :3])
+        blk = xc.at[0, e, y]
+        for to, _ in peers(i):
+            send(i, X2, blk, blk, dev(y_=to))
 
     def ag2c(i):
-        es = units(i)
-        got(i, C1, xc.at[1, es, :3, xx])
-        for j in (1, 2, 3):
-            blk = xc.at[1, es, :, xx]
-            send(i, C2, blk, blk, dev(x_=(xx + j) % 4))
+        e = CHUNKS[i][0]
+        got(i, C1, xc.at[1, e, heard(i), xx])
+        blk = xc.at[1, e, chips(i), xx]
+        for to, _ in across:
+            send(i, C2, blk, blk, dev(x_=to))
 
     def ready(_):
         for ld in loads[2:]:
             ld.wait()
 
     def gathered(i, k):
-        v = xc[k, units(i)].reshape(16 * SIZES[i], 16, HALF)
+        v = xc[k, CHUNKS[i][0], chips(i)].reshape(size[i] // 8, 16, HALF)
         v = unfold(v.astype(F32)).astype(BF16)
         xg[k, rows(i)] = v
         return v
 
     def mmx(i):
         rs = rows(i)
-        got(i, X2, xc.at[0, units(i), :3])
+        got(i, X2, xc.at[0, CHUNKS[i][0], heard(i)])
         xs = gathered(i, 0)
         for j, w in ((0, wg), (1, wu)):
             csnd[j, rs] = nn(xs, w[:, theirs])
@@ -184,7 +211,7 @@
 
     def mmc(i):
         rs = rows(i)
-        got(i, C2, xc.at[1, units(i), :3])
+        got(i, C2, xc.at[1, CHUNKS[i][0], slots(i), :3])
         cs = gathered(i, 1)
         csnd[2, rs] = nt(cs, wd[theirs, :])
         send(i, CORE, csnd.at[2, rs], crcv.at[2, rs], dev(a_=1 - a))
@@ -241,62 +268,62 @@
         send(i, GC, blk, blk, dev(a_=1 - a))
 
     def outa(i):
-        rs, es, n = rows(i), units(i), SIZES[i]
+        rs, e, ys = rows(i), CHUNKS[i][0], chips(i)
         got(i, GC, hid.at[:, rs, theirs])
-        p = fold(nn(hid[0, rs], wd[...])).reshape(n, 4, 4, 16, HALF)
-        pf[0, es] = p
-        psnd[0, es] = p.astype(BF16)
-        for j in (1, 2, 3):
-            to = (xx + j) % 4
-            send(i, O1, psnd.at[0, es, :, to], p1rcv.at[0, j - 1, es], dev(x_=to))
+        p = fold(nn(hid[0, rs], wd[...])).reshape(-1, 4, 16, HALF)
+        pf[0, e, ys] = p
+        psnd[0, e, ys] = p.astype(BF16)
+        for to, j in across:
+            send(i, O1, psnd.at[0, e, ys, to], p1rcv.at[0, j, e, slots(i)], dev(x_=to))
 
     def outb(i):
-        rs, es, n = rows(i), units(i), SIZES[i]
-        p = fold(nt(hid[1, rs], wg[...]) + nt(hid[2, rs], wu[...])).reshape(n, 4, 4, 16, HALF)
-        pf[1, es] = p
-        psnd[1, es] = p.astype(BF16)
-        for j in (1, 2, 3):
-            to = (y + j) % 4
-            send(i, G1, psnd.at[1, es, to], p1rcv.at[1, j - 1, es], dev(y_=to))
-
-    def second(i, k, t):
-        es = units(i)
+        rs, e, ys = rows(i), CHUNKS[i][0], chips(i)
+        p = fold(nt(hid[1, rs], wg[...]) + nt(hid[2, rs], wu[...])).reshape(-1, 4, 16, HALF)
+        pf[1, e, ys] = p
+        psnd[1, e, ys] = p.astype(BF16)
+        for to, j in peers(i):
+            send(i, G1, psnd.at[1, e, to], p1rcv.at[1, j, e], dev(y_=to))
+
+    def o2a(i):
+        e, part = CHUNKS[i]
+        got(i, O1, p1rcv.at[0, :, e, slots(i)])
+        t = pf[0, e, chips(i), xx]
         for j in range(3):
-            t = t + p1rcv[k, j, es].astype(F32)
-        sf[:SIZES[i]] = t
-        s1snd[k, es] = t.astype(BF16)
-
-    def o2a(i):
-        es = units(i)
-        got(i, O1, p1rcv.at[0, :, es])
-        second(i, 0, pf[0, es, :, xx])
-        for j in (1, 2, 3):
-            to = (y + j) % 4
-            send(i, O2, s1snd.at[0, es, to], p2rcv.at[0, j - 1, es], dev(y_=to))
-        s1own[0, es] = sf[:SIZES[i], y]
-
-    def o2b(i):
-        es = units(i)
-        got(i, G1, p1rcv.at[1, :, es])
-        second(i, 1, pf[1, es, y])
-        for j in (1, 2, 3):
-            to = (xx + j) % 4
-            send(i, G2, s1snd.at[1, es, to], p2rcv.at[1, j - 1, es], dev(x_=to))
-        s1own[1, es] = sf[:SIZES[i], xx]
-
-    def third(i, k, kind):
-        es = units(i)
-        got(i, kind, p2rcv.at[k, :, es])
-        t = s1own[k, es]
+            t = t + p1rcv[0, j, e, slots(i)].astype(F32)
+        sf[slots(i)] = t
+        s1snd[0, e, slots(i)] = t.astype(BF16)
+        first = {WHOLE: 0, NEAR: here, FAR: there - 2}[part]
+        for to, j in peers(i):
+            send(i, O2, s1snd.at[0, e, to - first], p2rcv.at[0, j, e], dev(y_=to))
+        if part != FAR:
+            s1own[0, e] = sf[y - first]
+
+    def o2b(e):
+        for i in chunks(e):
+            got(i, G1, p1rcv.at[1, heard(i), e])
+        t = pf[1, e, y]
         for j in range(3):
-            t = t + p2rcv[k, j, es].astype(F32)
-        fin[k, es] = t
-
-    def o3a(i):
-        third(i, 0, O2)
-
-    def o3b(i):
-        third(i, 1, G2)
+            t = t + p1rcv[1, j, e].astype(F32)
+        sf[...] = t
+        s1snd[1, e] = t.astype(BF16)
+        for to, j in across:
+            send(chunks(e)[0], G2, s1snd.at[1, e, to], p2rcv.at[1, j, e], dev(x_=to))
+        s1own[1, e] = sf[xx]
+
+    def third(e, k):
+        t = s1own[k, e]
+        for j in range(3):
+            t = t + p2rcv[k, j, e].astype(F32)
+        fin[k, e] = t
+
+    def o3a(e):
+        for i in chunks(e):
+            got(i, O2, p2rcv.at[0, heard(i), e])
+        third(e, 0)
+
+    def o3b(e):
+        got(chunks(e)[0], G2, p2rcv.at[1, :, e])
+        third(e, 1)
 
     def fin_send(_):
         push(KINDS + 1, last + FIN, fin.at[:, OTHER[0]:OTHER[-1] + 1], frcv, dev(zl_=1 - zl))
@@ -407,7 +434,7 @@
             pltpu.VMEM((2, 6, 4, 4, 16, HALF), F32),
             pltpu.VMEM((2, 6, 4, 4, 16, HALF), BF16),
             pltpu.VMEM((2, 3, 6, 4, 16, HALF), BF16),
-            pltpu.VMEM((max(SIZES), 4, 16, HALF), F32),
+            pltpu.VMEM((4, 16, HALF), F32),
             pltpu.VMEM((2, 6, 4, 16, HALF), BF16),
             pltpu.VMEM((2, 6, 16, HALF), F32),
             pltpu.VMEM((2, 3, 6, 16, HALF), BF16),

time: 103 us -> 102 us (level)
  no operation moved by 1% of the time
where the time goes in v6:
time: 102 us
  Pallas kernels  101 us (99%)
    pallas_call x1, Pallas kernels, local(): pl.pallas_call(functools.partial(kernel, PLAN), name='swiglu', out_shape=...  98.1 us
    pallas_call x1, Pallas kernels, local(): pl.pallas_call(move, name='move', out_shape=(small, small, big, big, big)...  3 us

profile of v6, /device:TPU:32, one launch (start us, length us, event | category | flops | bytes accessed | tf_op | source)
XLA Modules:
  0.0 101.9 jit_solution(9975386241716966166)
XLA Ops:
  0.6 98.1 %swiglu.1 = (bf16[24,768]{1,0:T(8,128)(2,1)}, bf16[24,768]{1,0:T(8,128)(2,1)}, bf16[768,768]{1,0:T(8,128)(2,1)}, bf16[768,768]{1,0:T(8,128)(2,1)}, bf16[768,768]{1,0:T(8,128)(2,1)}) custom-call(bf16[24,768]{1,0:T(8,128)(2,1)} %x_hbm.1, bf16[24,768]{1,0:T(8,128)(2,1)} %c_hbm.1, bf16[768,768]{1,0:T(8,128)(2,1)} %wg_hbm.1, bf16[768,768]{1,0:T(8,128)(2,1)} %wu_hbm.1, ...), custom_call_target="tpu_custom_call" | custom-call | flops 8153726976 | bytes 7077888 | tf_op jit(solution)/shard_map/swiglu/pallas_call | solution.py:412
  98.7 3.0 %move.1 = (bf16[24,768]{1,0:T(8,128)(2,1)}, bf16[24,768]{1,0:T(8,128)(2,1)}, bf16[768,768]{1,0:T(8,128)(2,1)}, bf16[768,768]{1,0:T(8,128)(2,1)}, bf16[768,768]{1,0:T(8,128)(2,1)}) custom-call(bf16[24,768]{1,0:T(8,128)(2,1)} %get-tuple-element.10.refs_0_, bf16[24,768]{1,0:T(8,128)(2,1)} %get-tuple-element.11.refs_1_, ...), custom_call_target="tpu_custom_call" | custom-call | tf_op jit(solution)/shard_map/move/pallas_call | solution.py:453

commit v7 on v6

--- a/solution.py
+++ b/solution.py
@@ -24,8 +24,6 @@
 ZL, FIN = 0, 3
 SENDS = KINDS + 2
 RECVS = 14 * len(CHUNKS) + 2 * 6 + 4
-
-DIRECT = ()
 
 PLAN = (
     ("ag1", 0), ("zl_send", 2), ("ag1", 4), ("ag2x", 0), ("ag2c", 0), ("zl_send", 1),
@@ -87,7 +85,7 @@
     def dev(zl_=zl, y_=y, zh_=zh, a_=a, x_=xx):
         return (zl_ * 4 + y_, zh_ * 2 + a_, x_)
 
-    others = ([dev(zl_=1 - zl), dev(a_=1 - a), dev(zh_=nxt), dev(zh_=prv), dev(zh_=opp)]
+    others = ([dev(zl_=1 - zl), dev(a_=1 - a), dev(zh_=nxt), dev(zh_=prv)]
               + [dev(x_=(xx + j) % 4) for j in (1, 2, 3)]
               + [dev(y_=(y + j) % 4) for j in (1, 2, 3)])
     mine = pl.ds(pl.multiple_of(a * HALF, 128), HALF)
@@ -246,15 +244,12 @@
         blk = hid.at[:, ps, mine]
         send(i, GN, blk, blk, dev(zh_=nxt))
         send(i, GP, blk, blk, dev(zh_=prv))
-        if i in DIRECT:
-            send(i, GF, blk, blk, dev(zh_=opp))
         send(i, GC, blk, blk, dev(a_=1 - a))
 
     def fw(i):
         blk = hid.at[:, piece(i, prv), mine]
         got(i, GN, blk)
-        if i not in DIRECT:
-            send(i, GF, blk, blk, dev(zh_=nxt))
+        send(i, GF, blk, blk, dev(zh_=nxt))
         send(i, GC, blk, blk, dev(a_=1 - a))
 
     def fp(i):
@@ -354,7 +349,7 @@
                 grad[which, ds, :] = ((t + acc[which, ds, :]) * scale).astype(BF16)
             return _
 
-        lax.fori_loop(0, 3, tile, 0)
+        lax.fori_loop(0, 3, tile, 0, unroll=True)
         if i == 1:
             st = pltpu.make_async_copy(grad.at[which], res, gsem.at[which])
             st.start()

time: 102 us -> 100 us (0.980)
  Pallas kernels: 101 us -> 99.5 us
    pallas_call x1, Pallas kernels: 98.1 us -> 96.5 us  [local(): pl.pallas_call(functools.partial(kernel, PLAN), name='swiglu', out_shape=...]
where the time goes in v7:
time: 100 us
  Pallas kernels  99.5 us (100%)
    pallas_call x1, Pallas kernels, local(): pl.pallas_call(functools.partial(kernel, PLAN), name='swiglu', out_shape=...  96.5 us
    pallas_call x1, Pallas kernels, local(): pl.pallas_call(move, name='move', out_shape=(small, small, big, big, big)...  3 us

profile of v7, /device:TPU:32, one launch (start us, length us, event | category | flops | bytes accessed | tf_op | source)
XLA Modules:
  0.0 100.3 jit_solution(4515213045876519598)
XLA Ops:
  0.6 96.5 %swiglu.1 = (bf16[24,768]{1,0:T(8,128)(2,1)}, bf16[24,768]{1,0:T(8,128)(2,1)}, bf16[768,768]{1,0:T(8,128)(2,1)}, bf16[768,768]{1,0:T(8,128)(2,1)}, bf16[768,768]{1,0:T(8,128)(2,1)}) custom-call(bf16[24,768]{1,0:T(8,128)(2,1)} %x_hbm.1, bf16[24,768]{1,0:T(8,128)(2,1)} %c_hbm.1, bf16[768,768]{1,0:T(8,128)(2,1)} %wg_hbm.1, bf16[768,768]{1,0:T(8,128)(2,1)} %wu_hbm.1, ...), custom_call_target="tpu_custom_call" | custom-call | flops 8153726976 | bytes 7077888 | tf_op jit(solution)/shard_map/swiglu/pallas_call | solution.py:407
  97.2 3.0 %move.1 = (bf16[24,768]{1,0:T(8,128)(2,1)}, bf16[24,768]{1,0:T(8,128)(2,1)}, bf16[768,768]{1,0:T(8,128)(2,1)}, bf16[768,768]{1,0:T(8,128)(2,1)}, bf16[768,768]{1,0:T(8,128)(2,1)}) custom-call(bf16[24,768]{1,0:T(8,128)(2,1)} %get-tuple-element.10.refs_0_, bf16[24,768]{1,0:T(8,128)(2,1)} %get-tuple-element.11.refs_1_, ...), custom_call_target="tpu_custom_call" | custom-call | tf_op jit(solution)/shard_map/move/pallas_call | solution.py:448

commit v8 on v7

--- a/solution.py
+++ b/solution.py
@@ -23,7 +23,7 @@
 KINDS = 16
 ZL, FIN = 0, 3
 SENDS = KINDS + 2
-RECVS = 14 * len(CHUNKS) + 2 * 6 + 4
+RECVS = 13 * len(CHUNKS) + 2 * 6 + 4
 
 PLAN = (
     ("ag1", 0), ("zl_send", 2), ("ag1", 4), ("ag2x", 0), ("ag2c", 0), ("zl_send", 1),
@@ -228,12 +228,11 @@
         qs = quarter(i)
         got(i, ZA, zrcv.at[0, :, qs])
         zsnd[2, :, qs] = (part[:, piece(i, nxt)] + zrcv[0, :, qs].astype(F32)).astype(BF16)
-        send(i, ZC, zsnd.at[2, :, qs], zrcv.at[2, :, qs], dev(zh_=nxt))
+        push(ZC, at(i, ZB), zsnd.at[2, :, qs], zrcv.at[2, :, qs], dev(zh_=nxt))
 
     def el(i):
         qs, ps = quarter(i), piece(i, zh)
-        got(i, ZB, zrcv.at[1, :, qs])
-        got(i, ZC, zrcv.at[2, :, qs])
+        got(i, ZB, zrcv.at[1:, :, qs])
         tot = part[:, ps] + zrcv[1, :, qs].astype(F32) + zrcv[2, :, qs].astype(F32)
         gate, up, slope = tot[0], tot[1], tot[2]
         sig = 1.0 / (1.0 + jnp.exp(-gate))

time: 100 us -> 100 us (level)
  no operation moved by 1% of the time
where the time goes in v8:
time: 100 us
  Pallas kernels  99.5 us (100%)
    pallas_call x1, Pallas kernels, local(): pl.pallas_call(functools.partial(kernel, PLAN), name='swiglu', out_shape=...  96.5 us
    pallas_call x1, Pallas kernels, local(): pl.pallas_call(move, name='move', out_shape=(small, small, big, big, big)...  3 us

profile of v8, /device:TPU:32, one launch (start us, length us, event | category | flops | bytes accessed | tf_op | source)
XLA Modules:
  0.0 100.3 jit_solution(8549408217591180392)
XLA Ops:
  0.6 96.5 %swiglu.1 = (bf16[24,768]{1,0:T(8,128)(2,1)}, bf16[24,768]{1,0:T(8,128)(2,1)}, bf16[768,768]{1,0:T(8,128)(2,1)}, bf16[768,768]{1,0:T(8,128)(2,1)}, bf16[768,768]{1,0:T(8,128)(2,1)}) custom-call(bf16[24,768]{1,0:T(8,128)(2,1)} %x_hbm.1, bf16[24,768]{1,0:T(8,128)(2,1)} %c_hbm.1, bf16[768,768]{1,0:T(8,128)(2,1)} %wg_hbm.1, bf16[768,768]{1,0:T(8,128)(2,1)} %wu_hbm.1, ...), custom_call_target="tpu_custom_call" | custom-call | flops 8153726976 | bytes 7077888 | tf_op jit(solution)/shard_map/swiglu/pallas_call | solution.py:406
  97.1 3.0 %move.1 = (bf16[24,768]{1,0:T(8,128)(2,1)}, bf16[24,768]{1,0:T(8,128)(2,1)}, bf16[768,768]{1,0:T(8,128)(2,1)}, bf16[768,768]{1,0:T(8,128)(2,1)}, bf16[768,768]{1,0:T(8,128)(2,1)}) custom-call(bf16[24,768]{1,0:T(8,128)(2,1)} %get-tuple-element.10.refs_0_, bf16[24,768]{1,0:T(8,128)(2,1)} %get-tuple-element.11.refs_1_, ...), custom_call_target="tpu_custom_call" | custom-call | tf_op jit(solution)/shard_map/move/pallas_call | solution.py:447
